TPU v7x, 32 devices: a whole 2x2x4 slice. The times are simulated.
32 devices in a mesh: ctx: 16 (over z, y, core), grp: 2 (over x).
Axes of the slice: x: 2, y: 2, z: 4, core: 2. Of those that a mesh axis runs over, the one named last changes fastest.
Arguments:
- queries: bfloat16 [8192, 1024], P('ctx', 'grp'), may hold values from -6 to 6
- key_rows: bfloat16 [8192, 256], P('ctx', 'grp'), may hold values from -6 to 6
- value_rows: bfloat16 [8192, 256], P('ctx', 'grp'), may hold values from -6 to 6
- output_rows: bfloat16 [8192, 1024], P('ctx', 'grp'), may hold values from -6 to 6
- output_grad: bfloat16 [8192, 1024], P('ctx', 'grp'), may hold values from -6 to 6
- log_normalizer: float32 [8192, 8], P('ctx', 'grp'), may hold values from 4 to 6
- selection: int32 [16, 3], replicated, may hold values from 0 to 14, as said below
- query_weight: bfloat16 [4096, 1024], P(None, 'grp'), may hold values from -0.09375 to 0.09375
- key_weight: bfloat16 [4096, 256], P(None, 'grp'), may hold values from -0.09375 to 0.09375
- value_weight: bfloat16 [4096, 256], P(None, 'grp'), may hold values from -0.09375 to 0.09375
Outputs:
- input_grad: bfloat16 [8192, 4096], P('ctx', 'grp')
Inputs may be any that keep to these rules, and one draw needn't show every extreme that they name: `selection`: row b names the 3 blocks chosen for query block b: distinct blocks below b, among them always block b - 1; a row with fewer than 3 blocks below it names all of them and repeats b itself in the remaining places.
All inputs are finite; a program needn't handle non-finite values.
Results may differ from a plain program's by a relative error of at most 0.019.
Values may be sent and summed in bfloat16 or wider, within the bound.
A program may use at most 128 MiB of HBM per device.

v0:
```python
import jax
import jax.numpy as jnp
from jax import lax
from jax.sharding import PartitionSpec as P

HD = 128
BLOCK = 512
TOPK = 3


def shifted(block, axis, distance):
    devices = range(lax.axis_size(axis))
    route = [(i - distance, i) for i in devices if i - distance in devices]
    return lax.ppermute(block, axis, route)


def shifted_2(value, axis, steps):
    count = lax.axis_size(axis)
    pairs = [(source, (source + steps) % count) for source in range(count)]
    return lax.ppermute(value, axis, pairs)


def pair_mask(query_anchor, key_anchor, row_count, picked):
    offsets = jnp.arange(row_count, dtype=jnp.int32)
    query_pos = query_anchor * row_count + offsets
    key_pos = key_anchor * row_count + offsets
    query_block = query_pos // BLOCK
    key_block = key_pos // BLOCK
    causal = (query_block[:, None] == key_block[None, :]) & (key_pos[None, :] <= query_pos[:, None])
    block_ids = jnp.arange(picked.shape[0], dtype=jnp.int32)
    query_onehot = (query_block[:, None] == block_ids[None, :]).astype(jnp.float32)
    key_onehot = (key_block[:, None] == block_ids[None, :]).astype(jnp.float32)
    chosen = jnp.dot(jnp.dot(query_onehot, picked), key_onehot.T) > 0.5
    return causal | chosen


def gradients(query_side, key_side, allowed):
    query_in, grad_in, norm_in, delta_in = query_side
    key_in, value_in = key_side
    query_count = query_in.shape[0]
    key_count = key_in.shape[0]
    groups = key_in.shape[1] // HD
    per_group = query_in.shape[1] // (HD * groups)
    scaling = float(HD) ** (-0.5)
    query_heads = query_in.reshape(query_count, groups, per_group, HD)
    grad_heads = grad_in.reshape(query_count, groups, per_group, HD)
    key_heads = key_in.reshape(key_count, groups, HD)
    value_heads = value_in.reshape(key_count, groups, HD)
    norm_heads = norm_in.reshape(query_count, groups, per_group).transpose(1, 2, 0)[:, :, :, None]
    delta_heads = delta_in.reshape(query_count, groups, per_group).transpose(1, 2, 0)[:, :, :, None]
    scores = (
        jnp.einsum("qgpd,kgd->gpqk", query_heads, key_heads, preferred_element_type=jnp.float32)
        * scaling
    )
    probs = jnp.where(allowed[None, None], jnp.exp(scores - norm_heads), 0.0)
    prob_grad = jnp.einsum(
        "qgpd,kgd->gpqk", grad_heads, value_heads, preferred_element_type=jnp.float32
    )
    score_grad = probs * (prob_grad - delta_heads)
    probs_half = probs.astype(jnp.bfloat16)
    score_half = score_grad.astype(jnp.bfloat16)
    value_part = jnp.einsum(
        "gpqk,qgpd->kgd", probs_half, grad_heads, preferred_element_type=jnp.float32
    ).reshape(key_count, -1)
    key_part = jnp.einsum(
        "gpqk,qgpd->kgd", score_half, query_heads, preferred_element_type=jnp.float32
    ).reshape(key_count, -1)
    query_part = jnp.einsum(
        "gpqk,kgd->qgpd", score_half, key_heads, preferred_element_type=jnp.float32
    ).reshape(query_count, -1)
    return (query_part, key_part, value_part)


def guarded(query_side, key_side, allowed):

    def skipped():
        return (
            jnp.zeros(query_side[0].shape, jnp.float32),
            jnp.zeros(key_side[0].shape, jnp.float32),
            jnp.zeros(key_side[1].shape, jnp.float32),
        )

    return lax.cond(jnp.any(allowed), lambda: gradients(query_side, key_side, allowed), skipped)


def on_device(
    queries,
    key_rows,
    value_rows,
    output_rows,
    output_grad,
    log_normalizer,
    selection,
    query_weight,
    key_weight,
    value_weight,
):
    scaling = float(HD) ** (-0.5)
    row_count = queries.shape[0]
    head_count = queries.shape[1] // HD
    cycle_size = lax.axis_size("ctx")
    position = lax.axis_index("ctx")
    block_count = selection.shape[0]
    row_delta = jnp.sum(
        (output_rows.astype(jnp.float32) * output_grad.astype(jnp.float32)).reshape(
            row_count, head_count, HD
        ),
        axis=-1,
    )
    block_ids = jnp.arange(block_count, dtype=jnp.int32)
    picked = jnp.zeros((block_count, block_count), jnp.float32)
    for column in range(TOPK):
        picked = jnp.maximum(
            picked, (selection[:, column][:, None] == block_ids[None, :]).astype(jnp.float32)
        )
    picked = jnp.where(block_ids[None, :] < block_ids[:, None], picked, 0.0)
    query_side = (queries, output_grad, log_normalizer, row_delta)

    def key_turn(turn_index, state):
        travel_key, travel_value, key_total, value_total, query_total = state
        anchor = position - turn_index
        allowed = pair_mask(position, anchor, row_count, picked)
        query_part, key_part, value_part = guarded(query_side, (travel_key, travel_value), allowed)
        return (
            travel_key,
            travel_value,
            key_total + key_part,
            value_total + value_part,
            query_total + query_part,
        )

    def key_step(turn_index, state):
        state = key_turn(turn_index, state)
        travel_key, travel_value = shifted((state[0], state[1]), "ctx", 1)
        key_total, value_total = (
            shifted_2(state[2].astype(jnp.bfloat16), "ctx", 1).astype(jnp.float32),
            shifted_2(state[3].astype(jnp.bfloat16), "ctx", 1).astype(jnp.float32),
        )
        return (travel_key, travel_value, key_total, value_total, state[4])

    key_zero = jnp.zeros(key_rows.shape, jnp.float32)
    state = (key_rows, value_rows, key_zero, key_zero, jnp.zeros(queries.shape, jnp.float32))
    state = lax.fori_loop(0, cycle_size - 1, key_step, state)
    state = key_turn(cycle_size - 1, state)
    key_total, value_total = (
        shifted_2(state[2].astype(jnp.bfloat16), "ctx", 1).astype(jnp.float32),
        shifted_2(state[3].astype(jnp.bfloat16), "ctx", 1).astype(jnp.float32),
    )
    query_total = state[4]
    grad_query = (query_total * scaling).astype(jnp.bfloat16)
    grad_key = (key_total * scaling).astype(jnp.bfloat16)
    grad_value = value_total.astype(jnp.bfloat16)
    contract = (((1,), (1,)), ((), ()))
    combined = lax.dot_general(
        grad_query, query_weight, contract, preferred_element_type=jnp.float32
    )
    combined = combined + lax.dot_general(
        grad_key, key_weight, contract, preferred_element_type=jnp.float32
    )
    combined = combined + lax.dot_general(
        grad_value, value_weight, contract, preferred_element_type=jnp.float32
    )
    return lax.psum_scatter(combined.astype(jnp.bfloat16), "grp", scatter_dimension=1, tiled=True)


def solution(mesh):
    return jax.shard_map(
        on_device,
        mesh=mesh,
        in_specs=(
            P("ctx", "grp"),
            P("ctx", "grp"),
            P("ctx", "grp"),
            P("ctx", "grp"),
            P("ctx", "grp"),
            P("ctx", "grp"),
            P(),
            P(None, "grp"),
            P(None, "grp"),
            P(None, "grp"),
        ),
        out_specs=P("ctx", "grp"),
        check_vma=False,
    )
```

profile of v0, /device:TPU:0, one launch (start us, length us, event | category | flops | bytes accessed | tf_op | source)
XLA Modules:
  0.0 476.0 jit_solution(9569784967930917323)
XLA Ops:
  17.8 382.7 %while.25 = (s32[]{:T(128)}, bf16[512,128]{0,1:T(8,128)(2,1)S(1)}, bf16[512,128]{1,0:T(8,128)(2,1)}, f32[512,128]{1,0:T(8,128)}, f32[512,128]{1,0:T(8,128)}, /*i...) while((s32[]{:T(128)}, bf16[512,128]{0,1:T(8,128)(2,1)S(1)}, ...), condition=%wide.region_5.6_spmd.clone, body=%wide.region_1.5_spmd.clone.sunk | while | flops 1363970816 | bytes 38478580 | solution.py:143
  22.4 5.2 %collective-permute-start.1 = (bf16[512,128]{1,0:T(8,128)(2,1)}, bf16[512,128]{1,0:T(8,128)(2,1)}, u32[]{:S(2)}, u32[]{:S(2)}) collective-permute-start(bf16[512,128]{1,0:T(8,128)(2,1)} %copy.99), channel_id=1, source_target_pairs={{0,2},{2,4},{4,6},{6,8},{8,10},{10,12},{12,14},{14,16},{16,18},{18... | collective-permute-start | bytes 393224 | tf_op jit(solution)/shard_map/while/body/eval_jaxpr/ppermute | solution.py:14
  27.6 2.6 fusion.171
  30.9 9.6 %conditional.5 = (f32[512,512]{0,1:T(8,128)S(1)}, f32[512,128]{1,0:T(8,128)}, f32[512,128]{1,0:T(8,128)S(1)}) conditional(s32[]{:T(128)} %convert_element_type.224, () %tuple.85, (pred[512,512]{1,0:T(8,128)(4,1)}, bf16[512,512]{1,0:T(8,128)(2,1)}, bf16[512,128]{0,1:T(8,128)(2,1)}, f32[512,4]{0,1:T(4,128)}, bf16[512,512]{1,0:T(8,128)(2,1)}, ...), branch_computations={%region_3.3_spmd, %region_4.4_spmd} | conditional | flops 1352663040 | bytes 30335112 | solution.py:83
  44.2 4.3 collective-permute-done.3
  56.3 2.6 fusion.171
  62.1 7.7 %collective-permute-start.3 = (bf16[512,128]{1,0:T(8,128)(2,1)}, bf16[512,128]{1,0:T(8,128)(2,1)S(1)}, u32[]{:S(2)}, u32[]{:S(2)}) collective-permute-start(bf16[512,128]{1,0:T(8,128)(2,1)} %fusion.173), channel_id=1, source_target_pairs={{0,2},{2,4},{4,6},{6,8},{8,10},{10,12},{12,14},{14,16},{16,18},{18... | collective-permute-start | bytes 393224 | tf_op jit(solution)/shard_map/while/body/eval_jaxpr/ppermute | solution.py:20
  75.1 3.7 collective-permute-done.2
  83.0 3.0 collective-permute-start.1
  86.0 2.6 fusion.171
  93.5 9.8 %collective-permute-start.2 = (bf16[512,128]{1,0:T(8,128)(2,1)}, bf16[512,128]{1,0:T(8,128)(2,1)S(1)}, u32[]{:S(2)}, u32[]{:S(2)}) collective-permute-start(bf16[512,128]{1,0:T(8,128)(2,1)} %fusion.172), channel_id=1, source_target_pairs={{0,2},{2,4},{4,6},{6,8},{8,10},{10,12},{12,14},{14,16},{16,18},{18... | collective-permute-start | bytes 393224 | tf_op jit(solution)/shard_map/while/body/eval_jaxpr/ppermute | solution.py:20
  105.9 3.0 collective-permute-start
  110.4 4.9 %collective-permute-start.1 = (bf16[512,128]{1,0:T(8,128)(2,1)}, bf16[512,128]{1,0:T(8,128)(2,1)}, u32[]{:S(2)}, u32[]{:S(2)}) collective-permute-start(bf16[512,128]{1,0:T(8,128)(2,1)} %copy.99), channel_id=1, source_target_pairs={{0,2},{2,4},{4,6},{6,8},{8,10},{10,12},{12,14},{14,16},{16,18},{18... | collective-permute-start | bytes 393224 | tf_op jit(solution)/shard_map/while/body/eval_jaxpr/ppermute | solution.py:14
  115.3 2.6 fusion.171
  125.1 3.3 collective-permute-done.3
  131.5 7.5 %collective-permute-start = (bf16[512,128]{0,1:T(8,128)(2,1)}, bf16[512,128]{0,1:T(8,128)(2,1)S(1)}, u32[]{:S(2)}, u32[]{:S(2)}) collective-permute-start(bf16[512,128]{0,1:T(8,128)(2,1)} %copy.98), channel_id=1, source_target_pairs={{0,2},{2,4},{4,6},{6,8},{8,10},{10,12},{12,14},{14,16},{16,18},{18... | collective-permute-start | bytes 393224 | tf_op jit(solution)/shard_map/while/body/eval_jaxpr/ppermute | solution.py:14
  140.6 4.9 %collective-permute-start.1 = (bf16[512,128]{1,0:T(8,128)(2,1)}, bf16[512,128]{1,0:T(8,128)(2,1)}, u32[]{:S(2)}, u32[]{:S(2)}) collective-permute-start(bf16[512,128]{1,0:T(8,128)(2,1)} %copy.99), channel_id=1, source_target_pairs={{0,2},{2,4},{4,6},{6,8},{8,10},{10,12},{12,14},{14,16},{16,18},{18... | collective-permute-start | bytes 393224 | tf_op jit(solution)/shard_map/while/body/eval_jaxpr/ppermute | solution.py:14
  145.5 2.6 fusion.171
  153.6 4.9 %collective-permute-done.3 = bf16[512,128]{1,0:T(8,128)(2,1)S(1)} collective-permute-done((bf16[512,128]{1,0:T(8,128)(2,1)}, bf16[512,128]{1,0:T(8,128)(2,1)S(1)}, u32[]{:S(2)}, u32[]{:S(2)}) %collective-permute-start.3) | collective-permute-done | bytes 131104 | tf_op jit(solution)/shard_map/while/body/eval_jaxpr/ppermute | solution.py:20
  164.5 6.1 %collective-permute-start.1 = (bf16[512,128]{1,0:T(8,128)(2,1)}, bf16[512,128]{1,0:T(8,128)(2,1)}, u32[]{:S(2)}, u32[]{:S(2)}) collective-permute-start(bf16[512,128]{1,0:T(8,128)(2,1)} %copy.99), channel_id=1, source_target_pairs={{0,2},{2,4},{4,6},{6,8},{8,10},{10,12},{12,14},{14,16},{16,18},{18... | collective-permute-start | bytes 393224 | tf_op jit(solution)/shard_map/while/body/eval_jaxpr/ppermute | solution.py:14
  170.6 2.6 fusion.171
  178.6 3.2 collective-permute-start.2
  190.1 3.7 collective-permute-start.1
  193.8 2.6 fusion.171
  201.3 2.9 collective-permute-start.2
  212.8 4.5 collective-permute-start.1
  217.3 2.6 fusion.171
  227.8 3.1 collective-permute-done.3
  237.0 4.9 %collective-permute-start.1 = (bf16[512,128]{1,0:T(8,128)(2,1)}, bf16[512,128]{1,0:T(8,128)(2,1)}, u32[]{:S(2)}, u32[]{:S(2)}) collective-permute-start(bf16[512,128]{1,0:T(8,128)(2,1)} %copy.99), channel_id=1, source_target_pairs={{0,2},{2,4},{4,6},{6,8},{8,10},{10,12},{12,14},{14,16},{16,18},{18... | collective-permute-start | bytes 393224 | tf_op jit(solution)/shard_map/while/body/eval_jaxpr/ppermute | solution.py:14
  242.0 2.6 fusion.171
  258.1 5.9 %collective-permute-start = (bf16[512,128]{0,1:T(8,128)(2,1)}, bf16[512,128]{0,1:T(8,128)(2,1)S(1)}, u32[]{:S(2)}, u32[]{:S(2)}) collective-permute-start(bf16[512,128]{0,1:T(8,128)(2,1)} %copy.98), channel_id=1, source_target_pairs={{0,2},{2,4},{4,6},{6,8},{8,10},{10,12},{12,14},{14,16},{16,18},{18... | collective-permute-start | bytes 393224 | tf_op jit(solution)/shard_map/while/body/eval_jaxpr/ppermute | solution.py:14
  265.6 4.9 %collective-permute-start.1 = (bf16[512,128]{1,0:T(8,128)(2,1)}, bf16[512,128]{1,0:T(8,128)(2,1)}, u32[]{:S(2)}, u32[]{:S(2)}) collective-permute-start(bf16[512,128]{1,0:T(8,128)(2,1)} %copy.99), channel_id=1, source_target_pairs={{0,2},{2,4},{4,6},{6,8},{8,10},{10,12},{12,14},{14,16},{16,18},{18... | collective-permute-start | bytes 393224 | tf_op jit(solution)/shard_map/while/body/eval_jaxpr/ppermute | solution.py:14
  270.5 2.6 fusion.171
  289.5 3.1 collective-permute-start.1
  292.6 2.6 fusion.171
  300.6 3.2 collective-permute-start.2
  312.1 3.7 collective-permute-start.1
  315.8 2.6 fusion.171
  334.9 3.1 collective-permute-start.1
  346.1 4.9 %collective-permute-done.3 = bf16[512,128]{1,0:T(8,128)(2,1)S(1)} collective-permute-done((bf16[512,128]{1,0:T(8,128)(2,1)}, bf16[512,128]{1,0:T(8,128)(2,1)S(1)}, u32[]{:S(2)}, u32[]{:S(2)}) %collective-permute-start.3) | collective-permute-done | bytes 131104 | tf_op jit(solution)/shard_map/while/body/eval_jaxpr/ppermute | solution.py:20
  359.4 2.6 fusion.171
  378.4 4.0 collective-permute-start.1
  382.4 2.6 fusion.171
  392.5 3.2 collective-permute-start.2
  396.8 3.0 collective-permute-done.2
  402.6 5.0 %fusion.109 = f32[512,4096]{1,0:T(8,128)S(1)} fusion(bf16[4096,512]{1,0:T(8,128)(2,1)} %param.23, f32[512,512]{0,1:T(8,128)S(1)} %get-tuple-element.384, f32[512,512]{0,1:T(8,128)} %get-tuple-element.387), kind=kOutput, calls=%fused_computation.113 | convolution fusion | flops 2148270080 | bytes 14680064 | tf_op jit(solution)/shard_map/dot_general | solution.py:154
  410.5 3.2 add_convert_fusion
  413.7 55.4 %reduce-scatter.2.cloned.1.call-done = bf16[512,2048]{1,0:T(8,128)(2,1)} async-done(((bf16[512,4096]{1,0:T(8,128)(2,1)}), bf16[512,2048]{1,0:T(8,128)(2,1)}) %reduce-scatter.2.cloned.1.call-update) | async-done | bytes 2097168 | tf_op jit(solution)/shard_map/reduce_scatter | solution.py:163
  (335 shorter events, 234.8 us)
Async XLA Ops:
  6.5 462.6 %reduce-scatter.2.cloned.1.call-start = ((), (), s32[]{:S(2)}) async-start(), calls=%async_computation.1 | async-start | bytes 6291456 | tf_op jit(solution)/shard_map/reduce_scatter | solution.py:163
  18.5 32.4 %collective-permute-start = (bf16[512,128]{0,1:T(8,128)(2,1)}, bf16[512,128]{0,1:T(8,128)(2,1)S(1)}, u32[]{:S(2)}, u32[]{:S(2)}) collective-permute-start(bf16[512,128]{0,1:T(8,128)(2,1)} %copy.98), channel_id=1, source_target_pairs={{0,2},{2,4},{4,6},{6,8},{8,10},{10,12},{12,14},{14,16},{16,18},{18... | collective-permute-start | bytes 393224 | tf_op jit(solution)/shard_map/while/body/eval_jaxpr/ppermute | solution.py:14
  22.4 28.5 %collective-permute-start.1 = (bf16[512,128]{1,0:T(8,128)(2,1)}, bf16[512,128]{1,0:T(8,128)(2,1)}, u32[]{:S(2)}, u32[]{:S(2)}) collective-permute-start(bf16[512,128]{1,0:T(8,128)(2,1)} %copy.99), channel_id=1, source_target_pairs={{0,2},{2,4},{4,6},{6,8},{8,10},{10,12},{12,14},{14,16},{16,18},{18... | collective-permute-start | bytes 393224 | tf_op jit(solution)/shard_map/while/body/eval_jaxpr/ppermute | solution.py:14
  51.5 28.0 %collective-permute-start = (bf16[512,128]{0,1:T(8,128)(2,1)}, bf16[512,128]{0,1:T(8,128)(2,1)S(1)}, u32[]{:S(2)}, u32[]{:S(2)}) collective-permute-start(bf16[512,128]{0,1:T(8,128)(2,1)} %copy.98), channel_id=1, source_target_pairs={{0,2},{2,4},{4,6},{6,8},{8,10},{10,12},{12,14},{14,16},{16,18},{18... | collective-permute-start | bytes 393224 | tf_op jit(solution)/shard_map/while/body/eval_jaxpr/ppermute | solution.py:14
  54.4 25.2 %collective-permute-start.1 = (bf16[512,128]{1,0:T(8,128)(2,1)}, bf16[512,128]{1,0:T(8,128)(2,1)}, u32[]{:S(2)}, u32[]{:S(2)}) collective-permute-start(bf16[512,128]{1,0:T(8,128)(2,1)} %copy.99), channel_id=1, source_target_pairs={{0,2},{2,4},{4,6},{6,8},{8,10},{10,12},{12,14},{14,16},{16,18},{18... | collective-permute-start | bytes 393224 | tf_op jit(solution)/shard_map/while/body/eval_jaxpr/ppermute | solution.py:14
  62.1 12.3 %collective-permute-start.3 = (bf16[512,128]{1,0:T(8,128)(2,1)}, bf16[512,128]{1,0:T(8,128)(2,1)S(1)}, u32[]{:S(2)}, u32[]{:S(2)}) collective-permute-start(bf16[512,128]{1,0:T(8,128)(2,1)} %fusion.173), channel_id=1, source_target_pairs={{0,2},{2,4},{4,6},{6,8},{8,10},{10,12},{12,14},{14,16},{16,18},{18... | collective-permute-start | bytes 393224 | tf_op jit(solution)/shard_map/while/body/eval_jaxpr/ppermute | solution.py:20
  71.5 7.3 %collective-permute-start.2 = (bf16[512,128]{1,0:T(8,128)(2,1)}, bf16[512,128]{1,0:T(8,128)(2,1)S(1)}, u32[]{:S(2)}, u32[]{:S(2)}) collective-permute-start(bf16[512,128]{1,0:T(8,128)(2,1)} %fusion.172), channel_id=1, source_target_pairs={{0,2},{2,4},{4,6},{6,8},{8,10},{10,12},{12,14},{14,16},{16,18},{18... | collective-permute-start | bytes 393224 | tf_op jit(solution)/shard_map/while/body/eval_jaxpr/ppermute | solution.py:20
  80.2 25.0 %collective-permute-start = (bf16[512,128]{0,1:T(8,128)(2,1)}, bf16[512,128]{0,1:T(8,128)(2,1)S(1)}, u32[]{:S(2)}, u32[]{:S(2)}) collective-permute-start(bf16[512,128]{0,1:T(8,128)(2,1)} %copy.98), channel_id=1, source_target_pairs={{0,2},{2,4},{4,6},{6,8},{8,10},{10,12},{12,14},{14,16},{16,18},{18... | collective-permute-start | bytes 393224 | tf_op jit(solution)/shard_map/while/body/eval_jaxpr/ppermute | solution.py:14
  83.0 22.2 %collective-permute-start.1 = (bf16[512,128]{1,0:T(8,128)(2,1)}, bf16[512,128]{1,0:T(8,128)(2,1)}, u32[]{:S(2)}, u32[]{:S(2)}) collective-permute-start(bf16[512,128]{1,0:T(8,128)(2,1)} %copy.99), channel_id=1, source_target_pairs={{0,2},{2,4},{4,6},{6,8},{8,10},{10,12},{12,14},{14,16},{16,18},{18... | collective-permute-start | bytes 393224 | tf_op jit(solution)/shard_map/while/body/eval_jaxpr/ppermute | solution.py:14
  91.8 11.9 %collective-permute-start.3 = (bf16[512,128]{1,0:T(8,128)(2,1)}, bf16[512,128]{1,0:T(8,128)(2,1)S(1)}, u32[]{:S(2)}, u32[]{:S(2)}) collective-permute-start(bf16[512,128]{1,0:T(8,128)(2,1)} %fusion.173), channel_id=1, source_target_pairs={{0,2},{2,4},{4,6},{6,8},{8,10},{10,12},{12,14},{14,16},{16,18},{18... | collective-permute-start | bytes 393224 | tf_op jit(solution)/shard_map/while/body/eval_jaxpr/ppermute | solution.py:20
  93.5 11.0 %collective-permute-start.2 = (bf16[512,128]{1,0:T(8,128)(2,1)}, bf16[512,128]{1,0:T(8,128)(2,1)S(1)}, u32[]{:S(2)}, u32[]{:S(2)}) collective-permute-start(bf16[512,128]{1,0:T(8,128)(2,1)} %fusion.172), channel_id=1, source_target_pairs={{0,2},{2,4},{4,6},{6,8},{8,10},{10,12},{12,14},{14,16},{16,18},{18... | collective-permute-start | bytes 393224 | tf_op jit(solution)/shard_map/while/body/eval_jaxpr/ppermute | solution.py:20
  105.9 25.0 %collective-permute-start = (bf16[512,128]{0,1:T(8,128)(2,1)}, bf16[512,128]{0,1:T(8,128)(2,1)S(1)}, u32[]{:S(2)}, u32[]{:S(2)}) collective-permute-start(bf16[512,128]{0,1:T(8,128)(2,1)} %copy.98), channel_id=1, source_target_pairs={{0,2},{2,4},{4,6},{6,8},{8,10},{10,12},{12,14},{14,16},{16,18},{18... | collective-permute-start | bytes 393224 | tf_op jit(solution)/shard_map/while/body/eval_jaxpr/ppermute | solution.py:14
  110.4 20.4 %collective-permute-start.1 = (bf16[512,128]{1,0:T(8,128)(2,1)}, bf16[512,128]{1,0:T(8,128)(2,1)}, u32[]{:S(2)}, u32[]{:S(2)}) collective-permute-start(bf16[512,128]{1,0:T(8,128)(2,1)} %copy.99), channel_id=1, source_target_pairs={{0,2},{2,4},{4,6},{6,8},{8,10},{10,12},{12,14},{14,16},{16,18},{18... | collective-permute-start | bytes 393224 | tf_op jit(solution)/shard_map/while/body/eval_jaxpr/ppermute | solution.py:14
  131.5 29.5 %collective-permute-start = (bf16[512,128]{0,1:T(8,128)(2,1)}, bf16[512,128]{0,1:T(8,128)(2,1)S(1)}, u32[]{:S(2)}, u32[]{:S(2)}) collective-permute-start(bf16[512,128]{0,1:T(8,128)(2,1)} %copy.98), channel_id=1, source_target_pairs={{0,2},{2,4},{4,6},{6,8},{8,10},{10,12},{12,14},{14,16},{16,18},{18... | collective-permute-start | bytes 393224 | tf_op jit(solution)/shard_map/while/body/eval_jaxpr/ppermute | solution.py:14
  140.6 20.4 %collective-permute-start.1 = (bf16[512,128]{1,0:T(8,128)(2,1)}, bf16[512,128]{1,0:T(8,128)(2,1)}, u32[]{:S(2)}, u32[]{:S(2)}) collective-permute-start(bf16[512,128]{1,0:T(8,128)(2,1)} %copy.99), channel_id=1, source_target_pairs={{0,2},{2,4},{4,6},{6,8},{8,10},{10,12},{12,14},{14,16},{16,18},{18... | collective-permute-start | bytes 393224 | tf_op jit(solution)/shard_map/while/body/eval_jaxpr/ppermute | solution.py:14
  151.3 7.3 %collective-permute-start.3 = (bf16[512,128]{1,0:T(8,128)(2,1)}, bf16[512,128]{1,0:T(8,128)(2,1)S(1)}, u32[]{:S(2)}, u32[]{:S(2)}) collective-permute-start(bf16[512,128]{1,0:T(8,128)(2,1)} %fusion.173), channel_id=1, source_target_pairs={{0,2},{2,4},{4,6},{6,8},{8,10},{10,12},{12,14},{14,16},{16,18},{18... | collective-permute-start | bytes 393224 | tf_op jit(solution)/shard_map/while/body/eval_jaxpr/ppermute | solution.py:20
  153.0 7.3 %collective-permute-start.2 = (bf16[512,128]{1,0:T(8,128)(2,1)}, bf16[512,128]{1,0:T(8,128)(2,1)S(1)}, u32[]{:S(2)}, u32[]{:S(2)}) collective-permute-start(bf16[512,128]{1,0:T(8,128)(2,1)} %fusion.172), channel_id=1, source_target_pairs={{0,2},{2,4},{4,6},{6,8},{8,10},{10,12},{12,14},{14,16},{16,18},{18... | collective-permute-start | bytes 393224 | tf_op jit(solution)/shard_map/while/body/eval_jaxpr/ppermute | solution.py:20
  161.7 24.9 %collective-permute-start = (bf16[512,128]{0,1:T(8,128)(2,1)}, bf16[512,128]{0,1:T(8,128)(2,1)S(1)}, u32[]{:S(2)}, u32[]{:S(2)}) collective-permute-start(bf16[512,128]{0,1:T(8,128)(2,1)} %copy.98), channel_id=1, source_target_pairs={{0,2},{2,4},{4,6},{6,8},{8,10},{10,12},{12,14},{14,16},{16,18},{18... | collective-permute-start | bytes 393224 | tf_op jit(solution)/shard_map/while/body/eval_jaxpr/ppermute | solution.py:14
  164.5 22.1 %collective-permute-start.1 = (bf16[512,128]{1,0:T(8,128)(2,1)}, bf16[512,128]{1,0:T(8,128)(2,1)}, u32[]{:S(2)}, u32[]{:S(2)}) collective-permute-start(bf16[512,128]{1,0:T(8,128)(2,1)} %copy.99), channel_id=1, source_target_pairs={{0,2},{2,4},{4,6},{6,8},{8,10},{10,12},{12,14},{14,16},{16,18},{18... | collective-permute-start | bytes 393224 | tf_op jit(solution)/shard_map/while/body/eval_jaxpr/ppermute | solution.py:14
  176.4 7.3 %collective-permute-start.3 = (bf16[512,128]{1,0:T(8,128)(2,1)}, bf16[512,128]{1,0:T(8,128)(2,1)S(1)}, u32[]{:S(2)}, u32[]{:S(2)}) collective-permute-start(bf16[512,128]{1,0:T(8,128)(2,1)} %fusion.173), channel_id=1, source_target_pairs={{0,2},{2,4},{4,6},{6,8},{8,10},{10,12},{12,14},{14,16},{16,18},{18... | collective-permute-start | bytes 393224 | tf_op jit(solution)/shard_map/while/body/eval_jaxpr/ppermute | solution.py:20
  178.6 7.3 %collective-permute-start.2 = (bf16[512,128]{1,0:T(8,128)(2,1)}, bf16[512,128]{1,0:T(8,128)(2,1)S(1)}, u32[]{:S(2)}, u32[]{:S(2)}) collective-permute-start(bf16[512,128]{1,0:T(8,128)(2,1)} %fusion.172), channel_id=1, source_target_pairs={{0,2},{2,4},{4,6},{6,8},{8,10},{10,12},{12,14},{14,16},{16,18},{18... | collective-permute-start | bytes 393224 | tf_op jit(solution)/shard_map/while/body/eval_jaxpr/ppermute | solution.py:20
  187.2 22.1 %collective-permute-start = (bf16[512,128]{0,1:T(8,128)(2,1)}, bf16[512,128]{0,1:T(8,128)(2,1)S(1)}, u32[]{:S(2)}, u32[]{:S(2)}) collective-permute-start(bf16[512,128]{0,1:T(8,128)(2,1)} %copy.98), channel_id=1, source_target_pairs={{0,2},{2,4},{4,6},{6,8},{8,10},{10,12},{12,14},{14,16},{16,18},{18... | collective-permute-start | bytes 393224 | tf_op jit(solution)/shard_map/while/body/eval_jaxpr/ppermute | solution.py:14
  190.1 19.3 %collective-permute-start.1 = (bf16[512,128]{1,0:T(8,128)(2,1)}, bf16[512,128]{1,0:T(8,128)(2,1)}, u32[]{:S(2)}, u32[]{:S(2)}) collective-permute-start(bf16[512,128]{1,0:T(8,128)(2,1)} %copy.99), channel_id=1, source_target_pairs={{0,2},{2,4},{4,6},{6,8},{8,10},{10,12},{12,14},{14,16},{16,18},{18... | collective-permute-start | bytes 393224 | tf_op jit(solution)/shard_map/while/body/eval_jaxpr/ppermute | solution.py:14
  199.6 7.3 %collective-permute-start.3 = (bf16[512,128]{1,0:T(8,128)(2,1)}, bf16[512,128]{1,0:T(8,128)(2,1)S(1)}, u32[]{:S(2)}, u32[]{:S(2)}) collective-permute-start(bf16[512,128]{1,0:T(8,128)(2,1)} %fusion.173), channel_id=1, source_target_pairs={{0,2},{2,4},{4,6},{6,8},{8,10},{10,12},{12,14},{14,16},{16,18},{18... | collective-permute-start | bytes 393224 | tf_op jit(solution)/shard_map/while/body/eval_jaxpr/ppermute | solution.py:20
  201.3 7.3 %collective-permute-start.2 = (bf16[512,128]{1,0:T(8,128)(2,1)}, bf16[512,128]{1,0:T(8,128)(2,1)S(1)}, u32[]{:S(2)}, u32[]{:S(2)}) collective-permute-start(bf16[512,128]{1,0:T(8,128)(2,1)} %fusion.172), channel_id=1, source_target_pairs={{0,2},{2,4},{4,6},{6,8},{8,10},{10,12},{12,14},{14,16},{16,18},{18... | collective-permute-start | bytes 393224 | tf_op jit(solution)/shard_map/while/body/eval_jaxpr/ppermute | solution.py:20
  210.0 23.4 %collective-permute-start = (bf16[512,128]{0,1:T(8,128)(2,1)}, bf16[512,128]{0,1:T(8,128)(2,1)S(1)}, u32[]{:S(2)}, u32[]{:S(2)}) collective-permute-start(bf16[512,128]{0,1:T(8,128)(2,1)} %copy.98), channel_id=1, source_target_pairs={{0,2},{2,4},{4,6},{6,8},{8,10},{10,12},{12,14},{14,16},{16,18},{18... | collective-permute-start | bytes 393224 | tf_op jit(solution)/shard_map/while/body/eval_jaxpr/ppermute | solution.py:14
  212.8 20.6 %collective-permute-start.1 = (bf16[512,128]{1,0:T(8,128)(2,1)}, bf16[512,128]{1,0:T(8,128)(2,1)}, u32[]{:S(2)}, u32[]{:S(2)}) collective-permute-start(bf16[512,128]{1,0:T(8,128)(2,1)} %copy.99), channel_id=1, source_target_pairs={{0,2},{2,4},{4,6},{6,8},{8,10},{10,12},{12,14},{14,16},{16,18},{18... | collective-permute-start | bytes 393224 | tf_op jit(solution)/shard_map/while/body/eval_jaxpr/ppermute | solution.py:14
  223.1 7.8 %collective-permute-start.3 = (bf16[512,128]{1,0:T(8,128)(2,1)}, bf16[512,128]{1,0:T(8,128)(2,1)S(1)}, u32[]{:S(2)}, u32[]{:S(2)}) collective-permute-start(bf16[512,128]{1,0:T(8,128)(2,1)} %fusion.173), channel_id=1, source_target_pairs={{0,2},{2,4},{4,6},{6,8},{8,10},{10,12},{12,14},{14,16},{16,18},{18... | collective-permute-start | bytes 393224 | tf_op jit(solution)/shard_map/while/body/eval_jaxpr/ppermute | solution.py:20
  224.8 7.8 %collective-permute-start.2 = (bf16[512,128]{1,0:T(8,128)(2,1)}, bf16[512,128]{1,0:T(8,128)(2,1)S(1)}, u32[]{:S(2)}, u32[]{:S(2)}) collective-permute-start(bf16[512,128]{1,0:T(8,128)(2,1)} %fusion.172), channel_id=1, source_target_pairs={{0,2},{2,4},{4,6},{6,8},{8,10},{10,12},{12,14},{14,16},{16,18},{18... | collective-permute-start | bytes 393224 | tf_op jit(solution)/shard_map/while/body/eval_jaxpr/ppermute | solution.py:20
  234.1 23.4 %collective-permute-start = (bf16[512,128]{0,1:T(8,128)(2,1)}, bf16[512,128]{0,1:T(8,128)(2,1)S(1)}, u32[]{:S(2)}, u32[]{:S(2)}) collective-permute-start(bf16[512,128]{0,1:T(8,128)(2,1)} %copy.98), channel_id=1, source_target_pairs={{0,2},{2,4},{4,6},{6,8},{8,10},{10,12},{12,14},{14,16},{16,18},{18... | collective-permute-start | bytes 393224 | tf_op jit(solution)/shard_map/while/body/eval_jaxpr/ppermute | solution.py:14
  237.0 20.4 %collective-permute-start.1 = (bf16[512,128]{1,0:T(8,128)(2,1)}, bf16[512,128]{1,0:T(8,128)(2,1)}, u32[]{:S(2)}, u32[]{:S(2)}) collective-permute-start(bf16[512,128]{1,0:T(8,128)(2,1)} %copy.99), channel_id=1, source_target_pairs={{0,2},{2,4},{4,6},{6,8},{8,10},{10,12},{12,14},{14,16},{16,18},{18... | collective-permute-start | bytes 393224 | tf_op jit(solution)/shard_map/while/body/eval_jaxpr/ppermute | solution.py:14
  258.1 27.9 %collective-permute-start = (bf16[512,128]{0,1:T(8,128)(2,1)}, bf16[512,128]{0,1:T(8,128)(2,1)S(1)}, u32[]{:S(2)}, u32[]{:S(2)}) collective-permute-start(bf16[512,128]{0,1:T(8,128)(2,1)} %copy.98), channel_id=1, source_target_pairs={{0,2},{2,4},{4,6},{6,8},{8,10},{10,12},{12,14},{14,16},{16,18},{18... | collective-permute-start | bytes 393224 | tf_op jit(solution)/shard_map/while/body/eval_jaxpr/ppermute | solution.py:14
  265.6 20.4 %collective-permute-start.1 = (bf16[512,128]{1,0:T(8,128)(2,1)}, bf16[512,128]{1,0:T(8,128)(2,1)}, u32[]{:S(2)}, u32[]{:S(2)}) collective-permute-start(bf16[512,128]{1,0:T(8,128)(2,1)} %copy.99), channel_id=1, source_target_pairs={{0,2},{2,4},{4,6},{6,8},{8,10},{10,12},{12,14},{14,16},{16,18},{18... | collective-permute-start | bytes 393224 | tf_op jit(solution)/shard_map/while/body/eval_jaxpr/ppermute | solution.py:14
  286.7 21.9 %collective-permute-start = (bf16[512,128]{0,1:T(8,128)(2,1)}, bf16[512,128]{0,1:T(8,128)(2,1)S(1)}, u32[]{:S(2)}, u32[]{:S(2)}) collective-permute-start(bf16[512,128]{0,1:T(8,128)(2,1)} %copy.98), channel_id=1, source_target_pairs={{0,2},{2,4},{4,6},{6,8},{8,10},{10,12},{12,14},{14,16},{16,18},{18... | collective-permute-start | bytes 393224 | tf_op jit(solution)/shard_map/while/body/eval_jaxpr/ppermute | solution.py:14
  289.5 19.1 %collective-permute-start.1 = (bf16[512,128]{1,0:T(8,128)(2,1)}, bf16[512,128]{1,0:T(8,128)(2,1)}, u32[]{:S(2)}, u32[]{:S(2)}) collective-permute-start(bf16[512,128]{1,0:T(8,128)(2,1)} %copy.99), channel_id=1, source_target_pairs={{0,2},{2,4},{4,6},{6,8},{8,10},{10,12},{12,14},{14,16},{16,18},{18... | collective-permute-start | bytes 393224 | tf_op jit(solution)/shard_map/while/body/eval_jaxpr/ppermute | solution.py:14
  300.6 7.3 %collective-permute-start.2 = (bf16[512,128]{1,0:T(8,128)(2,1)}, bf16[512,128]{1,0:T(8,128)(2,1)S(1)}, u32[]{:S(2)}, u32[]{:S(2)}) collective-permute-start(bf16[512,128]{1,0:T(8,128)(2,1)} %fusion.172), channel_id=1, source_target_pairs={{0,2},{2,4},{4,6},{6,8},{8,10},{10,12},{12,14},{14,16},{16,18},{18... | collective-permute-start | bytes 393224 | tf_op jit(solution)/shard_map/while/body/eval_jaxpr/ppermute | solution.py:20
  309.3 22.1 %collective-permute-start = (bf16[512,128]{0,1:T(8,128)(2,1)}, bf16[512,128]{0,1:T(8,128)(2,1)S(1)}, u32[]{:S(2)}, u32[]{:S(2)}) collective-permute-start(bf16[512,128]{0,1:T(8,128)(2,1)} %copy.98), channel_id=1, source_target_pairs={{0,2},{2,4},{4,6},{6,8},{8,10},{10,12},{12,14},{14,16},{16,18},{18... | collective-permute-start | bytes 393224 | tf_op jit(solution)/shard_map/while/body/eval_jaxpr/ppermute | solution.py:14
  312.1 19.3 %collective-permute-start.1 = (bf16[512,128]{1,0:T(8,128)(2,1)}, bf16[512,128]{1,0:T(8,128)(2,1)}, u32[]{:S(2)}, u32[]{:S(2)}) collective-permute-start(bf16[512,128]{1,0:T(8,128)(2,1)} %copy.99), channel_id=1, source_target_pairs={{0,2},{2,4},{4,6},{6,8},{8,10},{10,12},{12,14},{14,16},{16,18},{18... | collective-permute-start | bytes 393224 | tf_op jit(solution)/shard_map/while/body/eval_jaxpr/ppermute | solution.py:14
  321.6 7.3 %collective-permute-start.3 = (bf16[512,128]{1,0:T(8,128)(2,1)}, bf16[512,128]{1,0:T(8,128)(2,1)S(1)}, u32[]{:S(2)}, u32[]{:S(2)}) collective-permute-start(bf16[512,128]{1,0:T(8,128)(2,1)} %fusion.173), channel_id=1, source_target_pairs={{0,2},{2,4},{4,6},{6,8},{8,10},{10,12},{12,14},{14,16},{16,18},{18... | collective-permute-start | bytes 393224 | tf_op jit(solution)/shard_map/while/body/eval_jaxpr/ppermute | solution.py:20
  332.0 21.5 %collective-permute-start = (bf16[512,128]{0,1:T(8,128)(2,1)}, bf16[512,128]{0,1:T(8,128)(2,1)S(1)}, u32[]{:S(2)}, u32[]{:S(2)}) collective-permute-start(bf16[512,128]{0,1:T(8,128)(2,1)} %copy.98), channel_id=1, source_target_pairs={{0,2},{2,4},{4,6},{6,8},{8,10},{10,12},{12,14},{14,16},{16,18},{18... | collective-permute-start | bytes 393224 | tf_op jit(solution)/shard_map/while/body/eval_jaxpr/ppermute | solution.py:14
  334.9 18.6 %collective-permute-start.1 = (bf16[512,128]{1,0:T(8,128)(2,1)}, bf16[512,128]{1,0:T(8,128)(2,1)}, u32[]{:S(2)}, u32[]{:S(2)}) collective-permute-start(bf16[512,128]{1,0:T(8,128)(2,1)} %copy.99), channel_id=1, source_target_pairs={{0,2},{2,4},{4,6},{6,8},{8,10},{10,12},{12,14},{14,16},{16,18},{18... | collective-permute-start | bytes 393224 | tf_op jit(solution)/shard_map/while/body/eval_jaxpr/ppermute | solution.py:14
  354.1 20.8 %collective-permute-start = (bf16[512,128]{0,1:T(8,128)(2,1)}, bf16[512,128]{0,1:T(8,128)(2,1)S(1)}, u32[]{:S(2)}, u32[]{:S(2)}) collective-permute-start(bf16[512,128]{0,1:T(8,128)(2,1)} %copy.98), channel_id=1, source_target_pairs={{0,2},{2,4},{4,6},{6,8},{8,10},{10,12},{12,14},{14,16},{16,18},{18... | collective-permute-start | bytes 393224 | tf_op jit(solution)/shard_map/while/body/eval_jaxpr/ppermute | solution.py:14
  357.0 17.9 %collective-permute-start.1 = (bf16[512,128]{1,0:T(8,128)(2,1)}, bf16[512,128]{1,0:T(8,128)(2,1)}, u32[]{:S(2)}, u32[]{:S(2)}) collective-permute-start(bf16[512,128]{1,0:T(8,128)(2,1)} %copy.99), channel_id=1, source_target_pairs={{0,2},{2,4},{4,6},{6,8},{8,10},{10,12},{12,14},{14,16},{16,18},{18... | collective-permute-start | bytes 393224 | tf_op jit(solution)/shard_map/while/body/eval_jaxpr/ppermute | solution.py:14
  375.6 24.9 %collective-permute-start = (bf16[512,128]{0,1:T(8,128)(2,1)}, bf16[512,128]{0,1:T(8,128)(2,1)S(1)}, u32[]{:S(2)}, u32[]{:S(2)}) collective-permute-start(bf16[512,128]{0,1:T(8,128)(2,1)} %copy.98), channel_id=1, source_target_pairs={{0,2},{2,4},{4,6},{6,8},{8,10},{10,12},{12,14},{14,16},{16,18},{18... | collective-permute-start | bytes 393224 | tf_op jit(solution)/shard_map/while/body/eval_jaxpr/ppermute | solution.py:14
  378.4 22.1 %collective-permute-start.1 = (bf16[512,128]{1,0:T(8,128)(2,1)}, bf16[512,128]{1,0:T(8,128)(2,1)}, u32[]{:S(2)}, u32[]{:S(2)}) collective-permute-start(bf16[512,128]{1,0:T(8,128)(2,1)} %copy.99), channel_id=1, source_target_pairs={{0,2},{2,4},{4,6},{6,8},{8,10},{10,12},{12,14},{14,16},{16,18},{18... | collective-permute-start | bytes 393224 | tf_op jit(solution)/shard_map/while/body/eval_jaxpr/ppermute | solution.py:14
  388.2 7.9 %collective-permute-start.3 = (bf16[512,128]{1,0:T(8,128)(2,1)}, bf16[512,128]{1,0:T(8,128)(2,1)S(1)}, u32[]{:S(2)}, u32[]{:S(2)}) collective-permute-start(bf16[512,128]{1,0:T(8,128)(2,1)} %fusion.173), channel_id=1, source_target_pairs={{0,2},{2,4},{4,6},{6,8},{8,10},{10,12},{12,14},{14,16},{16,18},{18... | collective-permute-start | bytes 393224 | tf_op jit(solution)/shard_map/while/body/eval_jaxpr/ppermute | solution.py:20
  401.7 7.3 %collective-permute-start.4 = (bf16[512,128]{1,0:T(8,128)(2,1)S(1)}, bf16[512,128]{1,0:T(8,128)(2,1)S(1)}, u32[]{:S(2)}, u32[]{:S(2)}) collective-permute-start(bf16[512,128]{1,0:T(8,128)(2,1)S(1)} %add_convert_fusion.2), channel_id=1, source_target_pairs={{0,2},{2,4},{4,6},{6,8},{8,10},{10,12},{12,14},{14,16},{16,18},{18... | collective-permute-start | bytes 393224 | tf_op jit(solution)/shard_map/ppermute | solution.py:20
  402.0 8.4 %collective-permute-start.5 = (bf16[512,128]{1,0:T(8,128)(2,1)S(1)}, bf16[512,128]{1,0:T(8,128)(2,1)S(1)}, u32[]{:S(2)}, u32[]{:S(2)}) collective-permute-start(bf16[512,128]{1,0:T(8,128)(2,1)S(1)} %add_convert_fusion.1), channel_id=1, source_target_pairs={{0,2},{2,4},{4,6},{6,8},{8,10},{10,12},{12,14},{14,16},{16,18},{18... | collective-permute-start | bytes 393224 | tf_op jit(solution)/shard_map/ppermute | solution.py:20
  (25 other events, 532.0 us)
Sparse Core Ops, SparseCore 0:
  413.8 55.2 reduce-scatter.1
where the time goes:
time: 478 us; the launch traced here: 476 us
  starting transfers between devices  147 us (31%)
  waiting for transfers between devices  113 us (24%)
  other arithmetic  79.5 us (17%)
  matrix products  58.9 us (12%)
  local copies, waits for them, and re-layouts  53.3 us (11%)
  between operations  14.1 us (3%)
  loops' own time  10.2 us (2%)
    ppermute x30, starting transfers between devices, shifted(): return lax.ppermute(block, axis, route)  93.4 us
    ppermute x32, waiting for transfers between devices, shifted_2(): return lax.ppermute(value, axis, pairs)  57.6 us
    reduce_scatter x1, waiting for transfers between devices, on_device(): lax.psum_scatter(combined.astype(jnp.bfloat16), 'grp', scatter_dimension=...  55.4 us
    ppermute x32, starting transfers between devices, shifted_2(): return lax.ppermute(value, axis, pairs)  53.5 us
    dot_general x16, matrix products, pair_mask(): chosen = jnp.dot(jnp.dot(query_onehot, picked), key_onehot.T) > 0.5  41.4 us
    while x30, local copies, waits for them, and re-layouts  33.1 us
    convert_element_type x15, other arithmetic, key_step(): state[2].astype(jnp.bfloat16)  25.7 us
    convert_element_type x15, other arithmetic, key_step(): state[3].astype(jnp.bfloat16)  23.7 us
  transfers between devices with their start and end apart: 63, of which 30 were waited for; matrix products, arithmetic and copies ran while one was open for 35% of the time, Pallas kernels for 0%

commit v1 on v0

v1 whole, which is shorter than its diff:
```python
import functools
import math

import jax
import jax.numpy as jnp
from jax import lax
from jax.experimental import pallas as pl
from jax.experimental.pallas import tpu as pltpu
from jax.sharding import PartitionSpec as P

HD = 128
BLOCK = 512
TOPK = 3
MESH = pl.DeviceIdType.MESH
SCALE = float(HD) ** (-0.5)
LOG2E = math.log2(math.e)
VMEM_LIMIT = 56 * 1024 * 1024
NT = (((1,), (1,)), ((), ()))
NN = (((1,), (0,)), ((), ()))


def place():
    me = lax.axis_index("ctx")
    return me, me // 4, (me // 2) % 2, me % 2


def sibling_of(me, core):
    return me + 1 - 2 * core


def beside(me, column):
    return me + 2 - 4 * column


def remote(src, dst, send, recv, target):
    return pltpu.make_async_remote_copy(
        src_ref=src, dst_ref=dst, send_sem=send, recv_sem=recv,
        device_id={"ctx": target}, device_id_type=MESH,
    )


def greet(target):
    pl.semaphore_signal(
        pltpu.get_barrier_semaphore(), inc=1, device_id={"ctx": target}, device_id_type=MESH
    )


def gather_kernel(planes, kv_ref, all_ref, own_sem, z_send, z_recv, y_send, y_recv, c_send, c_recv):
    me, z, y, c = place()
    sibling, side = sibling_of(me, c), beside(me, y)
    greet(sibling)
    greet(side)

    @pl.when(z > 0)
    def _():
        greet(me - 4)

    own = pltpu.make_async_copy(kv_ref, all_ref.at[z, c, y], own_sem)
    own.start()
    pl.semaphore_wait(pltpu.get_barrier_semaphore(), 2 + (z < planes - 1).astype(jnp.int32))

    def up(s):
        src = kv_ref if s == 0 else all_ref.at[z - s, c, y]
        return remote(src, all_ref.at[z - s, c, y], z_send.at[s], z_recv.at[s + 1], me + 4)

    def from_below(s):
        slot = all_ref.at[z - s, c, y]
        return remote(slot, slot, z_send.at[s], z_recv.at[s], me)

    def across(s):
        src = kv_ref if s == 0 else all_ref.at[z - s, c, y]
        return remote(src, all_ref.at[z - s, c, y], y_send.at[s], y_recv.at[s], side)

    def between(s):
        pair = all_ref.at[z - s, c]
        return remote(pair, pair, c_send.at[s], c_recv.at[s], sibling)

    for s in range(planes + 1):
        if s < planes:

            @pl.when(z >= s)
            def _(s=s):
                if s > 0:
                    from_below(s).wait_recv()
                if s < planes - 1:

                    @pl.when(z < planes - 1)
                    def _():
                        up(s).start()

                across(s).start()

        if s == 0:
            own.wait()
        else:

            @pl.when(z >= s - 1)
            def _(s=s):
                across(s - 1).wait_recv()
                between(s - 1).start()

    for s in range(planes):

        @pl.when(z >= s)
        def _(s=s):
            if s < planes - 1:

                @pl.when(z < planes - 1)
                def _():
                    up(s).wait_send()

            across(s).wait_send()
            between(s).wait()


def gather_blocks(kv, planes):
    shape = (planes, 2, 2) + kv.shape
    dma = pltpu.SemaphoreType.DMA
    return pl.pallas_call(
        functools.partial(gather_kernel, planes),
        out_shape=jax.ShapeDtypeStruct(shape, kv.dtype),
        in_specs=[pl.BlockSpec(memory_space=pl.ANY)],
        out_specs=pl.BlockSpec(memory_space=pl.ANY),
        scratch_shapes=[dma(())] + [dma((planes,))] * 6,
        compiler_params=pltpu.CompilerParams(collective_id=0, has_side_effects=True),
        name="gather_blocks",
    )(kv)


def attend_kernel(
    chosen_ref, usable_ref, q_ref, do_ref, o_ref, lse_ref, kv_ref,
    dq_ref, part_ref, delta, dq_sum,
):
    slot = pl.program_id(0)
    heads = q_ref.shape[1] // HD

    def columns(h):
        return slice(h * HD, (h + 1) * HD)

    @pl.when(slot == 0)
    def _():
        part_ref[...] = jnp.zeros_like(part_ref)
        dq_sum[...] = jnp.zeros_like(dq_sum)
        for h in range(heads):
            product = do_ref[:, columns(h)].astype(jnp.float32) * o_ref[:, columns(h)].astype(jnp.float32)
            delta[h : h + 1, :] = jnp.sum(product.T, axis=0, keepdims=True)

    def pair(diagonal):
        key = kv_ref[0, 0, 0, :, :HD]
        value = kv_ref[0, 0, 0, :, HD:]
        key_t = key.astype(jnp.float32).T.astype(jnp.bfloat16)
        if diagonal:
            key_pos = lax.broadcasted_iota(jnp.int32, (BLOCK, BLOCK), 0)
            query_pos = lax.broadcasted_iota(jnp.int32, (BLOCK, BLOCK), 1)
            seen = key_pos <= query_pos
        dk = jnp.zeros((BLOCK, HD), jnp.float32)
        dv = jnp.zeros((BLOCK, HD), jnp.float32)
        for h in range(heads):
            query, cotangent = q_ref[:, columns(h)], do_ref[:, columns(h)]
            scores = lax.dot_general(key, query, NT, preferred_element_type=jnp.float32)
            probs = jnp.exp2(scores * (SCALE * LOG2E) - lse_ref[h : h + 1, :] * LOG2E)
            if diagonal:
                probs = jnp.where(seen, probs, 0.0)
            prob_grad = lax.dot_general(value, cotangent, NT, preferred_element_type=jnp.float32)
            score_half = (probs * (prob_grad - delta[h : h + 1, :])).astype(jnp.bfloat16)
            probs_half = probs.astype(jnp.bfloat16)
            dv = dv + lax.dot_general(probs_half, cotangent, NN, preferred_element_type=jnp.float32)
            dk = dk + lax.dot_general(score_half, query, NN, preferred_element_type=jnp.float32)
            dq_sum[h] += lax.dot_general(key_t, score_half, NN, preferred_element_type=jnp.float32)
        block = chosen_ref[slot]
        at = (block // 4, block % 2, (block // 2) % 2)
        part_ref[at + (slice(None), slice(0, HD))] = (dk * SCALE).astype(jnp.bfloat16)
        part_ref[at + (slice(None), slice(HD, 2 * HD))] = dv.astype(jnp.bfloat16)

    @pl.when(slot == 0)
    def _():
        pair(True)

    @pl.when((slot > 0) & (usable_ref[slot] > 0))
    def _():
        pair(False)

    @pl.when(slot == TOPK)
    def _():
        for h in range(heads):
            dq_ref[:, columns(h)] = (dq_sum[h] * SCALE).T.astype(jnp.bfloat16)


def attend(chosen, usable, queries, output_grad, output_rows, lse, blocks):
    rows, width = queries.shape
    heads = width // HD
    whole = lambda s, chosen, usable: (0, 0)
    wide = pl.BlockSpec((rows, width), whole)
    return pl.pallas_call(
        attend_kernel,
        out_shape=(
            jax.ShapeDtypeStruct((rows, width), jnp.bfloat16),
            jax.ShapeDtypeStruct(blocks.shape, jnp.bfloat16),
        ),
        grid_spec=pltpu.PrefetchScalarGridSpec(
            num_scalar_prefetch=2,
            grid=(TOPK + 1,),
            in_specs=[
                wide, wide, wide,
                pl.BlockSpec((heads, rows), whole),
                pl.BlockSpec(
                    (1, 1, 1) + blocks.shape[3:],
                    lambda s, chosen, usable: (
                        chosen[s] // 4, chosen[s] % 2, (chosen[s] // 2) % 2, 0, 0,
                    ),
                ),
            ],
            out_specs=[wide, pl.BlockSpec(blocks.shape, lambda s, chosen, usable: (0,) * 5)],
            scratch_shapes=[
                pltpu.VMEM((heads, rows), jnp.float32),
                pltpu.VMEM((heads, HD, rows), jnp.float32),
            ],
        ),
        compiler_params=pltpu.CompilerParams(vmem_limit_bytes=VMEM_LIMIT),
        cost_estimate=pl.CostEstimate(flops=6 * 10**9, bytes_accessed=10 * 2**20, transcendentals=4 * 2**20),
        name="attend",
    )(chosen, usable, queries, output_grad, output_rows, lse, blocks)


def scatter_kernel(
    planes, part_ref, out_ref, c_in, y_in, z_in, y_out, z_out, held,
    z_send, z_recv, y_send, y_recv, c_send, c_recv,
):
    me, z, y, c = place()
    sibling, side = sibling_of(me, c), beside(me, y)
    greet(sibling)
    greet(side)

    @pl.when(z < planes - 1)
    def _():
        greet(me + 4)

    pl.semaphore_wait(pltpu.get_barrier_semaphore(), 2 + (z > 0).astype(jnp.int32))

    def between(t):
        return remote(part_ref.at[t, 1 - c], c_in.at[t], c_send.at[t], c_recv.at[t], sibling)

    def across(t):
        return remote(y_out.at[t], y_in.at[t], y_send.at[t], y_recv.at[t], side)

    def down(t):
        return remote(z_out.at[t], z_in.at[t], z_send.at[t], z_recv.at[t], me - 4)

    for t in range(planes):

        @pl.when(t <= z)
        def _(t=t):
            between(t).start()

    for t in range(planes):

        @pl.when(t <= z)
        def _(t=t):
            between(t).wait_recv()
            y_out[t] = (
                part_ref[t, c, 1 - y].astype(jnp.float32) + c_in[t, 1 - y].astype(jnp.float32)
            ).astype(jnp.bfloat16)
            across(t).start()
            held[t] = part_ref[t, c, y].astype(jnp.float32) + c_in[t, y].astype(jnp.float32)

    for t in range(planes):

        @pl.when(t <= z)
        def _(t=t):
            across(t).wait_recv()
            held[t] += y_in[t].astype(jnp.float32)

            @pl.when(z < planes - 1)
            def _():
                down(t).wait_recv()
                held[t] += z_in[t].astype(jnp.float32)

            @pl.when(t < z)
            def _():
                z_out[t] = held[t].astype(jnp.bfloat16)
                down(t).start()

            @pl.when(t == z)
            def _():
                out_ref[...] = held[t].astype(jnp.bfloat16)

    for t in range(planes):

        @pl.when(t <= z)
        def _(t=t):
            between(t).wait_send()
            across(t).wait_send()

            @pl.when(t < z)
            def _():
                down(t).wait_send()


def scatter_blocks(part, planes):
    block = part.shape[3:]
    dma = pltpu.SemaphoreType.DMA
    slots = pltpu.VMEM((planes,) + block, jnp.bfloat16)
    return pl.pallas_call(
        functools.partial(scatter_kernel, planes),
        out_shape=jax.ShapeDtypeStruct(block, jnp.bfloat16),
        in_specs=[pl.BlockSpec(memory_space=pltpu.VMEM)],
        out_specs=pl.BlockSpec(memory_space=pltpu.VMEM),
        scratch_shapes=[
            pltpu.VMEM((planes, 2) + block, jnp.bfloat16),
            slots, slots, slots, slots,
            pltpu.VMEM((planes,) + block, jnp.float32),
        ] + [dma((planes,))] * 6,
        compiler_params=pltpu.CompilerParams(
            collective_id=1, has_side_effects=True, vmem_limit_bytes=VMEM_LIMIT
        ),
        cost_estimate=pl.CostEstimate(flops=10**9, bytes_accessed=100 * 2**20, transcendentals=0),
        name="scatter_blocks",
    )(part)


TILE = 256


def project_kernel(
    where_ref, dq_ref, dkv_ref, dq_far_ref, dkv_far_ref, wq_ref, wk_ref, wv_ref, near_ref, far_ref, out_ref
):
    step, half = pl.program_id(0), pl.num_programs(0) // 2
    feature = dq_ref.shape[1]

    def dot(lhs, rhs):
        return lax.dot_general(lhs, rhs, NT, preferred_element_type=jnp.float32)

    total = dot(dq_ref[...], wq_ref[...])
    total += dot(dkv_ref[:, :HD], wk_ref[...])
    total += dot(dkv_ref[:, HD:], wv_ref[...])
    weights = jnp.where(step < half, near_ref[...], far_ref[...])
    total += dot(dq_far_ref[...], weights[:, :feature])
    total += dot(dkv_far_ref[...], weights[:, feature:])
    out_ref[...] = total.astype(jnp.bfloat16)


def project(dq, dkv, dq_far, dkv_far, wq, wk, wv, near, far):
    rows = dq.shape[0]
    half = near.shape[0] // TILE
    where = jnp.stack([lax.axis_index("grp"), lax.axis_index("ctx") % 2]).astype(jnp.int32)

    def column(i, where):
        core = jnp.where(i < half, where[1], 1 - where[1])
        return core * half + i % half

    def whole(array):
        return pl.BlockSpec(array.shape, lambda i, where: (0, 0))

    def mine(array):
        return pl.BlockSpec(
            (TILE, array.shape[1]), lambda i, where: (where[0] * 2 * half + column(i, where), 0)
        )

    return pl.pallas_call(
        project_kernel,
        out_shape=jax.ShapeDtypeStruct((rows, 2 * half * TILE), jnp.bfloat16),
        grid_spec=pltpu.PrefetchScalarGridSpec(
            num_scalar_prefetch=1,
            grid=(2 * half,),
            in_specs=[
                whole(dq), whole(dkv), whole(dq_far), whole(dkv_far), mine(wq), mine(wk), mine(wv),
                pl.BlockSpec((TILE, near.shape[1]), lambda i, where: (jnp.minimum(i, half - 1), 0)),
                pl.BlockSpec((TILE, near.shape[1]), lambda i, where: (jnp.maximum(i - half, 0), 0)),
            ],
            out_specs=pl.BlockSpec((rows, TILE), lambda i, where: (0, column(i, where))),
        ),
        compiler_params=pltpu.CompilerParams(vmem_limit_bytes=VMEM_LIMIT),
        name="project",
    )(where, dq, dkv, dq_far, dkv_far, wq, wk, wv, near, far)


def on_device(
    queries, key_rows, value_rows, output_rows, output_grad, log_normalizer,
    selection, query_weight, key_weight, value_weight,
):
    position = lax.axis_index("ctx")
    contexts = lax.axis_size("ctx")
    groups = lax.axis_size("grp")
    planes = contexts // 4
    paired = groups == 2

    if paired:
        group, core = lax.axis_index("grp"), position % 2
        share = query_weight.shape[0] // 4
        start = (1 - group) * 2 * share + core * share
        swap = [(0, 1), (1, 0)]
        siblings = [(i, i ^ 1) for i in range(contexts)]
        outgoing = jnp.concatenate(
            [
                lax.dynamic_slice_in_dim(weight, start, share, 0)
                for weight in (query_weight, key_weight, value_weight)
            ],
            axis=1,
        )
        near = lax.ppermute(outgoing, "grp", swap)
        far = lax.ppermute(near, "ctx", siblings)

    blocks = gather_blocks(jnp.concatenate([key_rows, value_rows], axis=1), planes)
    row = lax.dynamic_index_in_dim(selection, position, 0, keepdims=False).astype(jnp.int32)
    chosen = jnp.concatenate([position[None].astype(jnp.int32), row])
    usable = jnp.concatenate([jnp.ones((1,), jnp.int32), (row < position).astype(jnp.int32)])
    grad_query, part = attend(
        chosen, usable, queries, output_grad, output_rows, log_normalizer.T, blocks
    )
    if paired:
        query_far = lax.ppermute(grad_query, "grp", swap)
    grad_keyval = scatter_blocks(part, planes)
    if paired:
        keyval_far = lax.ppermute(grad_keyval, "grp", swap)
        return project(
            grad_query, grad_keyval, query_far, keyval_far,
            query_weight, key_weight, value_weight, near, far,
        )
    dot = functools.partial(lax.dot_general, dimension_numbers=NT, preferred_element_type=jnp.float32)
    combined = dot(grad_query, query_weight)
    combined = combined + dot(grad_keyval[:, :HD], key_weight)
    combined = combined + dot(grad_keyval[:, HD:], value_weight)
    return lax.psum_scatter(combined.astype(jnp.bfloat16), "grp", scatter_dimension=1, tiled=True)


def solution(mesh):
    return jax.shard_map(
        on_device,
        mesh=mesh,
        in_specs=(
            P("ctx", "grp"),
            P("ctx", "grp"),
            P("ctx", "grp"),
            P("ctx", "grp"),
            P("ctx", "grp"),
            P("ctx", "grp"),
            P(),
            P(None, "grp"),
            P(None, "grp"),
            P(None, "grp"),
        ),
        out_specs=P("ctx", "grp"),
        check_vma=False,
    )
```

time: 478 us -> 150 us (0.31)
  starting transfers between devices: 147 us -> 5.11 us
  Pallas kernels: 0 us -> 97 us
  other arithmetic: 79.5 us -> 2.77 us
  waiting for transfers between devices: 113 us -> 40.1 us
  matrix products: 58.9 us -> 0 us
  local copies, waits for them, and re-layouts: 53.3 us -> 4.63 us
  between operations: 14.1 us -> 0.07 us
  loops' own time: 10.2 us -> 0 us
    ppermute x62 -> x4, starting transfers between devices: 147 us -> 5.11 us  [the longest x1 3.01 us: on_device(): near = lax.ppermute(outgoing, 'grp', swap)]
    pallas_call x0 -> x4, Pallas kernels: none -> 97 us  [the longest x1 66.4 us: scatter_blocks(): pl.pallas_call(functools.partial(scatter_kernel, planes), out_shape=jax.S...]
    convert_element_type x62 -> x0, other arithmetic: 70.9 us -> none  [the longest x15 25.7 us: key_step(): state[2].astype(jnp.bfloat16)]
    dot_general x24 -> x0, matrix products: 58.9 us -> none  [the longest x16 41.4 us: pair_mask(): chosen = jnp.dot(jnp.dot(query_onehot, picked), key_onehot.T) > 0.5]
    reduce_scatter x1 -> x0, waiting for transfers between devices: 55.4 us -> none  [on_device(): lax.psum_scatter(combined.astype(jnp.bfloat16), 'grp', scatter_dimension=...]
    while x30 -> x0, local copies, waits for them, and re-layouts: 33.1 us -> none
    ppermute x62 -> x4, waiting for transfers between devices: 57.7 us -> 40.1 us  [the longest x1 34.4 us: on_device(): near = lax.ppermute(outgoing, 'grp', swap)]
    another operation x46 -> x0, local copies, waits for them, and re-layouts: 14.3 us -> none
  transfers between devices with their start and end apart: 63 -> 4, of which waited for: 30 -> 2; matrix products, arithmetic and copies ran while one was open for 35% -> 2% of each run, Pallas kernels for 0% -> 58%
where the time goes in v1:
time: 150 us
  Pallas kernels  97 us (65%)
  waiting for transfers between devices  40.1 us (27%)
  starting transfers between devices  5.11 us (3%)
  local copies, waits for them, and re-layouts  4.63 us (3%)
  other arithmetic  2.77 us (2%)
    pallas_call x1, Pallas kernels, scatter_blocks(): pl.pallas_call(functools.partial(scatter_kernel, planes), out_shape=jax.S...  66.4 us
    ppermute x1, waiting for transfers between devices, on_device(): near = lax.ppermute(outgoing, 'grp', swap)  34.4 us
    pallas_call x1, Pallas kernels, gather_blocks(): pl.pallas_call(functools.partial(gather_kernel, planes), out_shape=jax.Sh...  12.4 us
    pallas_call x1, Pallas kernels, project(): pl.pallas_call(project_kernel, out_shape=jax.ShapeDtypeStruct((rows, 2 *...  10.4 us
    pallas_call x1, Pallas kernels, attend(): pl.pallas_call(attend_kernel, out_shape=(jax.ShapeDtypeStruct((rows, widt...  7.86 us
    ppermute x1, waiting for transfers between devices, on_device(): keyval_far = lax.ppermute(grad_keyval, 'grp', swap)  5.74 us
    ppermute x1, starting transfers between devices, on_device(): near = lax.ppermute(outgoing, 'grp', swap)  3.01 us
  transfers between devices with their start and end apart: 4, of which 2 were waited for; matrix products, arithmetic and copies ran while one was open for 2% of the time, Pallas kernels for 58%

profile of v1, /device:TPU:0, one launch (start us, length us, event | category | flops | bytes accessed | tf_op | source)
XLA Modules:
  0.0 149.7 jit_solution(16785597182853155303)
XLA Ops:
  0.0 0.0 copy-start
  0.0 0.0 copy-start.5
  0.0 0.0 copy-start.6
  0.0 1.3 constant_dynamic-slice_fusion.2
  1.3 1.1 constant_dynamic-slice_fusion
  2.4 0.1 pad_maximum_fusion
  2.6 3.0 %collective-permute-start.2 = (bf16[1024,768]{1,0:T(8,128)(2,1)S(1)}, bf16[1024,768]{1,0:T(8,128)(2,1)S(1)}, u32[]{:S(2)}, u32[]{:S(2)}) collective-permute-start(bf16[1024,768]{1,0:T(8,128)(2,1)S(1)} %pad_maximum_fusion), channel_id=1, source_target_pairs={{0,1},{1,0},{2,3},{3,2},{4,5},{5,4},{6,7},{7,6},{8,9},{9,8},{10,11... | collective-permute-start | bytes 4718600 | tf_op jit(solution)/shard_map/ppermute | solution.py:400
  5.6 34.4 %collective-permute-done.2.near_ref = bf16[1024,768]{1,0:T(8,128)(2,1)S(1)} collective-permute-done((bf16[1024,768]{1,0:T(8,128)(2,1)S(1)}, bf16[1024,768]{1,0:T(8,128)(2,1)S(1)}, u32[]{:S(2)}, u32[]{:S(2)}) %collective-permute-start.2) | collective-permute-done | bytes 1572896 | tf_op jit(solution)/shard_map/ppermute | solution.py:400
  40.0 0.0 copy-start.1
  40.0 0.0 collective-permute-start.3
  40.0 0.0 copy-done.5
  40.0 0.0 copy-done.6
  40.0 0.8 pad_maximum_fusion.1.kv_ref
  40.8 12.4 %gather_blocks.1.kv_ref = bf16[4,2,2,512,256]{4,3,2,1,0:T(8,128)(2,1)} custom-call(bf16[512,256]{1,0:T(8,128)(2,1)} %pad_maximum_fusion.1.kv_ref), custom_call_target="tpu_custom_call" | custom-call | tf_op jit(solution)/shard_map/gather_blocks/pallas_call | solution.py:119
  53.2 0.0 copy-done
  53.2 0.2 dynamic-slice_reduce_fusion
  53.4 0.6 pad_add_fusion.1.chosen_ref
  54.0 0.6 add_convert_fusion.usable_ref
  54.6 7.9 %attend.1 = (bf16[512,512]{1,0:T(8,128)(2,1)}, bf16[4,2,2,512,256]{4,3,2,1,0:T(8,128)(2,1)}) custom-call(s32[4]{0:T(128)} %pad_add_fusion.1.chosen_ref, s32[4]{0:T(128)} %add_convert_fusion.usable_ref, bf16[512,512]{1,0:T(8,128)(2,1)} %q_ref.1, bf16[512,512]{1,0:T(8,128)(2,1)} %do_ref.1, bf16[512,512]{1,0:T(8,128)(2,1)} %o_ref.1, f32[4,512]{1,0:T(4,128)} %bitcast.4, ...), custom_call_target="tpu_custom_call" | custom-call | flops 6000000000 | bytes 10485760 | tf_op jit(solution)/shard_map/attend/pallas_call | solution.py:194
  62.5 0.0 copy-done.1
  62.5 1.5 %collective-permute-start = (bf16[512,512]{1,0:T(8,128)(2,1)}, bf16[512,512]{1,0:T(8,128)(2,1)S(1)}, u32[]{:S(2)}, u32[]{:S(2)}) collective-permute-start(bf16[512,512]{1,0:T(8,128)(2,1)} %get-tuple-element.7.dq_ref), channel_id=1, source_target_pairs={{0,1},{1,0},{2,3},{3,2},{4,5},{5,4},{6,7},{7,6},{8,9},{9,8},{10,11... | collective-permute-start | bytes 1572872 | tf_op jit(solution)/shard_map/ppermute | solution.py:411
  64.0 66.4 %scatter_blocks.1.dkv_ref = bf16[512,256]{1,0:T(8,128)(2,1)} custom-call(bf16[4,2,2,512,256]{4,3,2,1,0:T(8,128)(2,1)} %get-tuple-element.8.part_ref), custom_call_target="tpu_custom_call" | custom-call | flops 1000000000 | bytes 104857600 | tf_op jit(solution)/shard_map/scatter_blocks/pallas_call | solution.py:303
  130.3 0.6 collective-permute-start.1
  130.9 0.6 pad_add_fusion.where_ref
  131.5 5.7 %collective-permute-done.1.dkv_far_ref = bf16[512,256]{1,0:T(8,128)(2,1)S(1)} collective-permute-done((bf16[512,256]{1,0:T(8,128)(2,1)}, bf16[512,256]{1,0:T(8,128)(2,1)S(1)}, u32[]{:S(2)}, u32[]{:S(2)}) %collective-permute-start.1) | collective-permute-done | bytes 262176 | tf_op jit(solution)/shard_map/ppermute | solution.py:414
  137.3 0.0 copy-start.4
  137.3 0.0 collective-permute-done.dq_far_ref
  137.3 0.0 copy-start.3
  137.3 0.0 collective-permute-done.3.far_ref
  137.3 0.7 copy-done.4
  138.0 0.2 copy-done.3
  138.1 0.0 copy-start.2
  138.2 1.1 copy-done.2
  139.3 10.4 %project.1 = bf16[512,2048]{1,0:T(8,128)(2,1)} custom-call(s32[2]{0:T(128)} %pad_add_fusion.where_ref, bf16[512,512]{1,0:T(8,128)(2,1)} %get-tuple-element.7.dq_ref, bf16[512,256]{1,0:T(8,128)(2,1)} %scatter_blocks.1.dkv_ref, bf16[512,512]{1,0:T(8,128)(2,1)} %copy-done.3, bf16[512,256]{1,0:T(8,128)(2,1)} %copy-done.4, bf16[4096,512]{1,0:T(8,128)(2,1)} %wq_ref.1, ...), custom_call_target="tpu_custom_call" | custom-call | tf_op jit(solution)/shard_map/project/pallas_call | solution.py:359
  (1 shorter events, 0.0 us)
Async XLA Ops:
  0.0 53.2 %copy-start = (s32[16,3]{0,1:T(4,128)S(1)}, s32[16,3]{0,1:T(4,128)}, u32[]{:S(2)}) copy-start(s32[16,3]{0,1:T(4,128)} %param.16) | copy-start | bytes 580
  0.0 40.0 %copy-start.5 = (bf16[512,128]{1,0:T(8,128)(2,1)S(1)}, bf16[512,128]{1,0:T(8,128)(2,1)}, u32[]{:S(2)}) copy-start(bf16[512,128]{1,0:T(8,128)(2,1)} %param.12) | copy-start | bytes 393220
  0.0 40.0 %copy-start.6 = (bf16[512,128]{1,0:T(8,128)(2,1)S(1)}, bf16[512,128]{1,0:T(8,128)(2,1)}, u32[]{:S(2)}) copy-start(bf16[512,128]{1,0:T(8,128)(2,1)} %param.11) | copy-start | bytes 393220
  2.6 37.4 %collective-permute-start.2 = (bf16[1024,768]{1,0:T(8,128)(2,1)S(1)}, bf16[1024,768]{1,0:T(8,128)(2,1)S(1)}, u32[]{:S(2)}, u32[]{:S(2)}) collective-permute-start(bf16[1024,768]{1,0:T(8,128)(2,1)S(1)} %pad_maximum_fusion), channel_id=1, source_target_pairs={{0,1},{1,0},{2,3},{3,2},{4,5},{5,4},{6,7},{7,6},{8,9},{9,8},{10,11... | collective-permute-start | bytes 4718600 | tf_op jit(solution)/shard_map/ppermute | solution.py:400
  40.0 22.5 %copy-start.1 = (bf16[1024,768]{1,0:T(8,128)(2,1)}, bf16[1024,768]{1,0:T(8,128)(2,1)S(1)}, u32[]{:S(2)}) copy-start(bf16[1024,768]{1,0:T(8,128)(2,1)S(1)} %collective-permute-done.2.near_ref) | copy-start | bytes 4718596
  40.0 97.3 %collective-permute-start.3 = (bf16[1024,768]{1,0:T(8,128)(2,1)S(1)}, bf16[1024,768]{1,0:T(8,128)(2,1)S(1)}, u32[]{:S(2)}, u32[]{:S(2)}) collective-permute-start(bf16[1024,768]{1,0:T(8,128)(2,1)S(1)} %collective-permute-done.2.near_ref), channel_id=1, source_target_pairs={{0,2},{2,0},{4,6},{6,4},{8,10},{10,8},{12,14},{14,12},{16,18},{18,... | collective-permute-start | bytes 4718600 | tf_op jit(solution)/shard_map/ppermute | solution.py:401
  62.5 74.8 %collective-permute-start = (bf16[512,512]{1,0:T(8,128)(2,1)}, bf16[512,512]{1,0:T(8,128)(2,1)S(1)}, u32[]{:S(2)}, u32[]{:S(2)}) collective-permute-start(bf16[512,512]{1,0:T(8,128)(2,1)} %get-tuple-element.7.dq_ref), channel_id=1, source_target_pairs={{0,1},{1,0},{2,3},{3,2},{4,5},{5,4},{6,7},{7,6},{8,9},{9,8},{10,11... | collective-permute-start | bytes 1572872 | tf_op jit(solution)/shard_map/ppermute | solution.py:411
  130.3 6.9 %collective-permute-start.1 = (bf16[512,256]{1,0:T(8,128)(2,1)}, bf16[512,256]{1,0:T(8,128)(2,1)S(1)}, u32[]{:S(2)}, u32[]{:S(2)}) collective-permute-start(bf16[512,256]{1,0:T(8,128)(2,1)} %scatter_blocks.1.dkv_ref), channel_id=1, source_target_pairs={{0,1},{1,0},{2,3},{3,2},{4,5},{5,4},{6,7},{7,6},{8,9},{9,8},{10,11... | collective-permute-start | bytes 786440 | tf_op jit(solution)/shard_map/ppermute | solution.py:414
  137.3 0.7 copy-start.4
  137.3 0.9 copy-start.3
  138.1 1.2 copy-start.2

commit v2 on v1

--- a/solution.py
+++ b/solution.py
@@ -318,60 +318,435 @@
     )(part)
 
 
+def toward(src, dst, send, recv):
+    return pltpu.make_async_remote_copy(
+        src_ref=src, dst_ref=dst, send_sem=send, recv_sem=recv,
+        device_id={"grp": 1 - lax.axis_index("grp")}, device_id_type=MESH,
+    )
+
+
+def greet_group():
+    pl.semaphore_signal(
+        pltpu.get_barrier_semaphore(), inc=1,
+        device_id={"grp": 1 - lax.axis_index("grp")}, device_id_type=MESH,
+    )
+
+
+def columns(h):
+    return slice(h * HD, (h + 1) * HD)
+
+
+def block_gradients(key, value, q_ref, do_ref, lse_ref, delta_ref, dq_sum, diagonal):
+    heads = q_ref.shape[1] // HD
+    key_t = key.astype(jnp.float32).T.astype(jnp.bfloat16)
+    if diagonal:
+        key_pos = lax.broadcasted_iota(jnp.int32, (BLOCK, BLOCK), 0)
+        query_pos = lax.broadcasted_iota(jnp.int32, (BLOCK, BLOCK), 1)
+        seen = key_pos <= query_pos
+    dk = jnp.zeros((BLOCK, HD), jnp.float32)
+    dv = jnp.zeros((BLOCK, HD), jnp.float32)
+    for h in range(heads):
+        query, cotangent = q_ref[:, columns(h)], do_ref[:, columns(h)]
+        scores = lax.dot_general(key, query, NT, preferred_element_type=jnp.float32)
+        probs = jnp.exp2(scores * (SCALE * LOG2E) - lse_ref[h : h + 1, :] * LOG2E)
+        if diagonal:
+            probs = jnp.where(seen, probs, 0.0)
+        prob_grad = lax.dot_general(value, cotangent, NT, preferred_element_type=jnp.float32)
+        score_half = (probs * (prob_grad - delta_ref[h : h + 1, :])).astype(jnp.bfloat16)
+        probs_half = probs.astype(jnp.bfloat16)
+        dv = dv + lax.dot_general(probs_half, cotangent, NN, preferred_element_type=jnp.float32)
+        dk = dk + lax.dot_general(score_half, query, NN, preferred_element_type=jnp.float32)
+        dq = lax.dot_general(key_t, score_half, NN, preferred_element_type=jnp.float32)
+        dq_sum[h] = dq if diagonal else dq_sum[h] + dq
+    return (dk * SCALE).astype(jnp.bfloat16), dv.astype(jnp.bfloat16)
+
+
+def open_kernel(
+    planes, key_ref, value_ref, q_ref, do_ref, o_ref, lse_ref, wq_ref, wk_ref, wv_ref,
+    all_ref, near_ref, dq_ref, delta_ref, known_ref,
+    kv, prev, own_sem, prev_sem, w_send, w_recv, z_send, z_recv, y_send, y_recv, c_send, c_recv,
+):
+    me, z, y, c = place()
+    group = lax.axis_index("grp")
+    sibling, side = sibling_of(me, c), beside(me, y)
+    greet(sibling)
+    greet(side)
+    greet_group()
+
+    @pl.when(z > 0)
+    def _():
+        greet(me - 4)
+
+    kv[0] = key_ref[...]
+    kv[1] = value_ref[...]
+    own = pltpu.make_async_copy(kv, all_ref.at[z, c, y], own_sem)
+    own.start()
+    pl.semaphore_wait(pltpu.get_barrier_semaphore(), 3 + (z < planes - 1).astype(jnp.int32))
+
+    share = near_ref.shape[0]
+    rows = pl.ds(pl.multiple_of((1 - group) * 2 * share + c * share, share), share)
+    weights = []
+    first = 0
+    for i, weight in enumerate((wq_ref, wk_ref, wv_ref)):
+        width = weight.shape[1]
+        weights.append(
+            toward(weight.at[rows], near_ref.at[:, first : first + width], w_send.at[i], w_recv.at[i])
+        )
+        first += width
+
+    def up(s):
+        src = kv if s == 0 else all_ref.at[z - s, c, y]
+        return remote(src, all_ref.at[z - s, c, y], z_send.at[s], z_recv.at[s + 1], me + 4)
+
+    def from_below(s):
+        slot = all_ref.at[z - s, c, y]
+        return remote(slot, slot, z_send.at[s], z_recv.at[s], me)
+
+    def across(s):
+        src = kv if s == 0 else all_ref.at[z - s, c, y]
+        return remote(src, all_ref.at[z - s, c, y], y_send.at[s], y_recv.at[s], side)
+
+    def between(s):
+        pair = all_ref.at[z - s, c]
+        return remote(pair, pair, c_send.at[s], c_recv.at[s], sibling)
+
+    for s in range(planes + 1):
+        if s < planes:
+
+            @pl.when(z >= s)
+            def _(s=s):
+                if s > 0:
+                    from_below(s).wait_recv()
+                if s < planes - 1:
+
+                    @pl.when(z < planes - 1)
+                    def _():
+                        up(s).start()
+
+                across(s).start()
+
+        if s == 0:
+            for copy in weights:
+                copy.start()
+            for h in range(q_ref.shape[1] // HD):
+                product = do_ref[:, columns(h)].astype(jnp.float32) * o_ref[:, columns(h)].astype(jnp.float32)
+                delta_ref[h : h + 1, :] = jnp.sum(product.T, axis=0, keepdims=True)
+            dk, dv = block_gradients(kv[0], kv[1], q_ref, do_ref, lse_ref, delta_ref, dq_ref, True)
+            known_ref[0, 0] = dk
+            known_ref[0, 1] = dv
+            own.wait()
+        else:
+
+            @pl.when(z >= s - 1)
+            def _(s=s):
+                across(s - 1).wait_recv()
+                between(s - 1).start()
+
+        if s == 2:
+            between(0).wait_recv()
+
+            @pl.when(z >= 1)
+            def _():
+                between(1).wait_recv()
+
+            @pl.when(me > 0)
+            def _():
+                last = me - 1
+                fetch = pltpu.make_async_copy(
+                    all_ref.at[last // 4, last % 2, (last // 2) % 2], prev, prev_sem
+                )
+                fetch.start()
+                fetch.wait()
+                dk, dv = block_gradients(prev[0], prev[1], q_ref, do_ref, lse_ref, delta_ref, dq_ref, False)
+                known_ref[1, 0] = dk
+                known_ref[1, 1] = dv
+
+    for s in range(planes):
+
+        @pl.when(z >= s)
+        def _(s=s):
+            if s < planes - 1:
+
+                @pl.when(z < planes - 1)
+                def _():
+                    up(s).wait_send()
+
+            across(s).wait_send()
+            between(s).wait_send()
+            if s > 1:
+                between(s).wait_recv()
+
+    for copy in weights:
+        copy.wait()
+
+
+def open_blocks(key, value, queries, output_grad, output_rows, lse, weights, planes):
+    rows, width = queries.shape
+    heads = width // HD
+    block = (2,) + key.shape
+    share = (weights[0].shape[0] // 4, sum(weight.shape[1] for weight in weights))
+    dma = pltpu.SemaphoreType.DMA
+    vmem = pl.BlockSpec(memory_space=pltpu.VMEM)
+    anywhere = pl.BlockSpec(memory_space=pl.ANY)
+    return pl.pallas_call(
+        functools.partial(open_kernel, planes),
+        out_shape=(
+            jax.ShapeDtypeStruct((planes, 2, 2) + block, jnp.bfloat16),
+            jax.ShapeDtypeStruct(share, jnp.bfloat16),
+            jax.ShapeDtypeStruct((heads, HD, rows), jnp.float32),
+            jax.ShapeDtypeStruct((heads, rows), jnp.float32),
+            jax.ShapeDtypeStruct((2,) + block, jnp.bfloat16),
+        ),
+        in_specs=[vmem] * 6 + [anywhere] * 3,
+        out_specs=(anywhere, anywhere, vmem, vmem, vmem),
+        scratch_shapes=[
+            pltpu.VMEM(block, jnp.bfloat16), pltpu.VMEM(block, jnp.bfloat16),
+            dma(()), dma(()), dma((3,)), dma((3,)),
+        ] + [dma((planes,))] * 6,
+        compiler_params=pltpu.CompilerParams(
+            collective_id=2, has_side_effects=True, vmem_limit_bytes=VMEM_LIMIT
+        ),
+        name="open_blocks",
+    )(key, value, queries, output_grad, output_rows, lse, *weights)
+
+
+def chosen_kernel(
+    selection_ref, q_ref, do_ref, lse_ref, delta_ref, dq_in_ref, known_ref, all_ref,
+    dq_ref, part_ref, fetched, dq_sum, sems,
+):
+    me = lax.axis_index("ctx")
+    picks = [selection_ref[me, column] for column in range(TOPK)]
+    others = [
+        jnp.where(picks[0] == me - 1, picks[1], picks[0]),
+        jnp.where(picks[2] == me - 1, picks[1], picks[2]),
+    ]
+
+    def at(block):
+        return (block // 4, block % 2, (block // 2) % 2)
+
+    copies = [
+        pltpu.make_async_copy(all_ref.at[at(block)], fetched.at[i], sems.at[i])
+        for i, block in enumerate(others)
+    ]
+    for copy in copies:
+        copy.start()
+    part_ref[...] = jnp.zeros_like(part_ref)
+    dq_sum[...] = dq_in_ref[...]
+    part_ref[at(me)] = known_ref[0]
+
+    @pl.when(me > 0)
+    def _():
+        part_ref[at(me - 1)] = known_ref[1]
+
+    for i, block in enumerate(others):
+        copies[i].wait()
+
+        @pl.when(block < me)
+        def _(i=i, block=block):
+            dk, dv = block_gradients(
+                fetched[i, 0], fetched[i, 1], q_ref, do_ref, lse_ref, delta_ref, dq_sum, False
+            )
+            part_ref[at(block) + (0,)] = dk
+            part_ref[at(block) + (1,)] = dv
+
+    for h in range(q_ref.shape[1] // HD):
+        dq_ref[:, columns(h)] = (dq_sum[h] * SCALE).T.astype(jnp.bfloat16)
+
+
+def chosen_blocks(selection, queries, output_grad, lse, delta, dq, known, blocks):
+    vmem = pl.BlockSpec(memory_space=pltpu.VMEM)
+    return pl.pallas_call(
+        chosen_kernel,
+        out_shape=(
+            jax.ShapeDtypeStruct(queries.shape, jnp.bfloat16),
+            jax.ShapeDtypeStruct(blocks.shape, jnp.bfloat16),
+        ),
+        in_specs=[pl.BlockSpec(memory_space=pltpu.SMEM)] + [vmem] * 6 + [pl.BlockSpec(memory_space=pl.ANY)],
+        out_specs=(vmem, vmem),
+        scratch_shapes=[
+            pltpu.VMEM((2,) + blocks.shape[3:], jnp.bfloat16),
+            pltpu.VMEM(dq.shape, jnp.float32),
+            pltpu.SemaphoreType.DMA((2,)),
+        ],
+        compiler_params=pltpu.CompilerParams(vmem_limit_bytes=VMEM_LIMIT),
+        name="chosen_blocks",
+    )(selection, queries, output_grad, lse, delta, dq, known, blocks)
+
+
 TILE = 256
 
 
-def project_kernel(
-    where_ref, dq_ref, dkv_ref, dq_far_ref, dkv_far_ref, wq_ref, wk_ref, wv_ref, near_ref, far_ref, out_ref
+def close_kernel(
+    planes, part_ref, dq_ref, near_ref, wq_ref, wk_ref, wv_ref, out_ref,
+    c_in, y_in, z_in, y_out, z_out, held, mine, theirs, dq_far, dkv, dkv_far, total,
+    z_send, z_recv, y_send, y_recv, c_send, c_recv, local_sem, w_send, w_recv, x_send, x_recv,
 ):
-    step, half = pl.program_id(0), pl.num_programs(0) // 2
+    me, z, y, c = place()
+    group = lax.axis_index("grp")
+    sibling, side = sibling_of(me, c), beside(me, y)
+    greet(sibling)
+    greet(side)
+    greet_group()
+
+    @pl.when(z < planes - 1)
+    def _():
+        greet(me + 4)
+
+    half = out_ref.shape[1]
+    share = half // 2
     feature = dq_ref.shape[1]
+    rows = pl.ds(pl.multiple_of(group * half, half), half)
+    locals_ = [pltpu.make_async_copy(near_ref, theirs.at[c], local_sem.at[0])]
+    first = 0
+    for i, weight in enumerate((wq_ref, wk_ref, wv_ref)):
+        width = weight.shape[1]
+        locals_.append(
+            pltpu.make_async_copy(weight.at[rows], mine.at[:, first : first + width], local_sem.at[i + 1])
+        )
+        first += width
+    for copy in locals_:
+        copy.start()
+
+    pl.semaphore_wait(pltpu.get_barrier_semaphore(), 3 + (z > 0).astype(jnp.int32))
+
+    def between(t):
+        return remote(part_ref.at[t, 1 - c], c_in.at[t], c_send.at[t], c_recv.at[t], sibling)
+
+    def across(t):
+        return remote(y_out.at[t], y_in.at[t], y_send.at[t], y_recv.at[t], side)
+
+    def down(t):
+        return remote(z_out.at[t], z_in.at[t], z_send.at[t], z_recv.at[t], me - 4)
+
+    query_swap = toward(dq_ref, dq_far, x_send.at[0], x_recv.at[0])
+    keyval_swap = toward(dkv, dkv_far, x_send.at[1], x_recv.at[1])
+    weight_swap = remote(near_ref, theirs.at[c], w_send, w_recv, sibling)
+
+    for t in range(planes):
+
+        @pl.when(t <= z)
+        def _(t=t):
+            between(t).start()
+
+    query_swap.start()
+    weight_swap.start()
+
+    for t in range(planes):
+
+        @pl.when(t <= z)
+        def _(t=t):
+            between(t).wait_recv()
+            y_out[t] = (
+                part_ref[t, c, 1 - y].astype(jnp.float32) + c_in[t, 1 - y].astype(jnp.float32)
+            ).astype(jnp.bfloat16)
+            across(t).start()
+            held[t] = part_ref[t, c, y].astype(jnp.float32) + c_in[t, y].astype(jnp.float32)
 
     def dot(lhs, rhs):
         return lax.dot_general(lhs, rhs, NT, preferred_element_type=jnp.float32)
 
-    total = dot(dq_ref[...], wq_ref[...])
-    total += dot(dkv_ref[:, :HD], wk_ref[...])
-    total += dot(dkv_ref[:, HD:], wv_ref[...])
-    weights = jnp.where(step < half, near_ref[...], far_ref[...])
-    total += dot(dq_far_ref[...], weights[:, :feature])
-    total += dot(dkv_far_ref[...], weights[:, feature:])
-    out_ref[...] = total.astype(jnp.bfloat16)
-
-
-def project(dq, dkv, dq_far, dkv_far, wq, wk, wv, near, far):
-    rows = dq.shape[0]
-    half = near.shape[0] // TILE
-    where = jnp.stack([lax.axis_index("grp"), lax.axis_index("ctx") % 2]).astype(jnp.int32)
-
-    def column(i, where):
-        core = jnp.where(i < half, where[1], 1 - where[1])
-        return core * half + i % half
-
-    def whole(array):
-        return pl.BlockSpec(array.shape, lambda i, where: (0, 0))
-
-    def mine(array):
-        return pl.BlockSpec(
-            (TILE, array.shape[1]), lambda i, where: (where[0] * 2 * half + column(i, where), 0)
-        )
-
+    def tiles(body):
+        @pl.loop(0, half // TILE)
+        def _(j):
+            here = pl.ds(pl.multiple_of(j * TILE, TILE), TILE)
+            there = (j * TILE // share, pl.ds(pl.multiple_of(j * TILE % share, TILE), TILE))
+            body(here, there)
+
+    for copy in locals_:
+        copy.wait()
+
+    def project_query(here, there):
+        total[:, here] = dot(dq_ref[...], mine[here, :feature])
+
+    tiles(project_query)
+
+    def project_query_far(here, there):
+        total[:, here] += dot(dq_far[...], theirs[there[0], there[1], :feature])
+
+    for t in range(planes):
+
+        @pl.when(t <= z)
+        def _(t=t):
+            @pl.when(t == z)
+            def _():
+                query_swap.wait()
+                weight_swap.wait()
+                tiles(project_query_far)
+
+            across(t).wait_recv()
+            held[t] += y_in[t].astype(jnp.float32)
+
+            @pl.when(z < planes - 1)
+            def _():
+                down(t).wait_recv()
+                held[t] += z_in[t].astype(jnp.float32)
+
+            @pl.when(t < z)
+            def _():
+                z_out[t] = held[t].astype(jnp.bfloat16)
+                down(t).start()
+
+            @pl.when(t == z)
+            def _():
+                dkv[:, :HD] = held[t, 0].astype(jnp.bfloat16)
+                dkv[:, HD:] = held[t, 1].astype(jnp.bfloat16)
+
+    keyval_swap.start()
+
+    def project_keyval(here, there):
+        total[:, here] += dot(dkv[...], mine[here, feature:])
+
+    tiles(project_keyval)
+    for t in range(planes):
+
+        @pl.when(t <= z)
+        def _(t=t):
+            between(t).wait_send()
+            across(t).wait_send()
+
+            @pl.when(t < z)
+            def _():
+                down(t).wait_send()
+
+    keyval_swap.wait()
+
+    def project_keyval_far(here, there):
+        out_ref[:, here] = (
+            total[:, here] + dot(dkv_far[...], theirs[there[0], there[1], feature:])
+        ).astype(jnp.bfloat16)
+
+    tiles(project_keyval_far)
+
+
+def close_blocks(part, dq, near, weights, planes):
+    block = part.shape[3:]
+    rows, width = dq.shape
+    half = 2 * near.shape[0]
+    dma = pltpu.SemaphoreType.DMA
+    slots = pltpu.VMEM((planes,) + block, jnp.bfloat16)
+    flat = pltpu.VMEM((rows, 2 * HD), jnp.bfloat16)
+    vmem = pl.BlockSpec(memory_space=pltpu.VMEM)
+    anywhere = pl.BlockSpec(memory_space=pl.ANY)
     return pl.pallas_call(
-        project_kernel,
-        out_shape=jax.ShapeDtypeStruct((rows, 2 * half * TILE), jnp.bfloat16),
-        grid_spec=pltpu.PrefetchScalarGridSpec(
-            num_scalar_prefetch=1,
-            grid=(2 * half,),
-            in_specs=[
-                whole(dq), whole(dkv), whole(dq_far), whole(dkv_far), mine(wq), mine(wk), mine(wv),
-                pl.BlockSpec((TILE, near.shape[1]), lambda i, where: (jnp.minimum(i, half - 1), 0)),
-                pl.BlockSpec((TILE, near.shape[1]), lambda i, where: (jnp.maximum(i - half, 0), 0)),
-            ],
-            out_specs=pl.BlockSpec((rows, TILE), lambda i, where: (0, column(i, where))),
+        functools.partial(close_kernel, planes),
+        out_shape=jax.ShapeDtypeStruct((rows, half), jnp.bfloat16),
+        in_specs=[vmem, vmem] + [anywhere] * 4,
+        out_specs=vmem,
+        scratch_shapes=[
+            pltpu.VMEM((planes, 2) + block, jnp.bfloat16),
+            slots, slots, slots, slots,
+            pltpu.VMEM((planes,) + block, jnp.float32),
+            pltpu.VMEM((half, near.shape[1]), jnp.bfloat16),
+            pltpu.VMEM((2,) + near.shape, jnp.bfloat16),
+            pltpu.VMEM(dq.shape, jnp.bfloat16),
+            flat, flat,
+            pltpu.VMEM((rows, half), jnp.float32),
+        ] + [dma((planes,))] * 6 + [dma((4,)), dma(()), dma(()), dma((2,)), dma((2,))],
+        compiler_params=pltpu.CompilerParams(
+            collective_id=3, has_side_effects=True, vmem_limit_bytes=VMEM_LIMIT
         ),
-        compiler_params=pltpu.CompilerParams(vmem_limit_bytes=VMEM_LIMIT),
-        name="project",
-    )(where, dq, dkv, dq_far, dkv_far, wq, wk, wv, near, far)
+        name="close_blocks",
+    )(part, dq, near, *weights)
 
 
 def on_device(
@@ -382,23 +757,16 @@
     contexts = lax.axis_size("ctx")
     groups = lax.axis_size("grp")
     planes = contexts // 4
-    paired = groups == 2
-
-    if paired:
-        group, core = lax.axis_index("grp"), position % 2
-        share = query_weight.shape[0] // 4
-        start = (1 - group) * 2 * share + core * share
-        swap = [(0, 1), (1, 0)]
-        siblings = [(i, i ^ 1) for i in range(contexts)]
-        outgoing = jnp.concatenate(
-            [
-                lax.dynamic_slice_in_dim(weight, start, share, 0)
-                for weight in (query_weight, key_weight, value_weight)
-            ],
-            axis=1,
+    if groups == 2:
+        weights = (query_weight, key_weight, value_weight)
+        lse = log_normalizer.T
+        blocks, near, dq, delta, known = open_blocks(
+            key_rows, value_rows, queries, output_grad, output_rows, lse, weights, planes
         )
-        near = lax.ppermute(outgoing, "grp", swap)
-        far = lax.ppermute(near, "ctx", siblings)
+        grad_query, part = chosen_blocks(
+            selection, queries, output_grad, lse, delta, dq, known, blocks
+        )
+        return close_blocks(part, grad_query, near, weights, planes)
 
     blocks = gather_blocks(jnp.concatenate([key_rows, value_rows], axis=1), planes)
     row = lax.dynamic_index_in_dim(selection, position, 0, keepdims=False).astype(jnp.int32)
@@ -407,15 +775,7 @@
     grad_query, part = attend(
         chosen, usable, queries, output_grad, output_rows, log_normalizer.T, blocks
     )
-    if paired:
-        query_far = lax.ppermute(grad_query, "grp", swap)
     grad_keyval = scatter_blocks(part, planes)
-    if paired:
-        keyval_far = lax.ppermute(grad_keyval, "grp", swap)
-        return project(
-            grad_query, grad_keyval, query_far, keyval_far,
-            query_weight, key_weight, value_weight, near, far,
-        )
     dot = functools.partial(lax.dot_general, dimension_numbers=NT, preferred_element_type=jnp.float32)
     combined = dot(grad_query, query_weight)
     combined = combined + dot(grad_keyval[:, :HD], key_weight)

time: 150 us -> 105 us (0.70)
  waiting for transfers between devices: 40.1 us -> 0 us
  starting transfers between devices: 5.11 us -> 0 us
  Pallas kernels: 97 us -> 100 us
  other arithmetic: 2.77 us -> 0 us
    ppermute x4 -> x0, waiting for transfers between devices: 40.1 us -> none  [the longest x1 34.4 us: on_device(): near = lax.ppermute(outgoing, 'grp', swap)]
    ppermute x4 -> x0, starting transfers between devices: 5.11 us -> none  [the longest x1 3.01 us: on_device(): near = lax.ppermute(outgoing, 'grp', swap)]
    pallas_call x4 -> x3, Pallas kernels: 97 us -> 100 us  [the longest x1 52.8 us: close_blocks(): pl.pallas_call(functools.partial(close_kernel, planes), out_shape=jax.Sha...]
    dynamic_slice x3 -> x0, local copies, waits for them, and re-layouts: 2.6 us -> none  [the longest x2 2.41 us: on_device(): lax.dynamic_slice_in_dim(weight, start, share, 0)]
    unnamed x14 -> x2, local copies, waits for them, and re-layouts: 2.03 us -> 4.51 us
    concatenate x4 -> x0, other arithmetic: 2.17 us -> none  [the longest x1 0.84 us: on_device(): jnp.concatenate([key_rows, value_rows], axis=1)]
  transfers between devices with their start and end apart: 4 -> 0, of which waited for: 2 -> 0; matrix products, arithmetic and copies ran while one was open for 2% -> 0% of each run, Pallas kernels for 58% -> 0%
where the time goes in v2:
time: 105 us
  Pallas kernels  100 us (95%)
  local copies, waits for them, and re-layouts  4.51 us (4%)
    pallas_call x1, Pallas kernels, close_blocks(): pl.pallas_call(functools.partial(close_kernel, planes), out_shape=jax.Sha...  52.8 us
    pallas_call x1, Pallas kernels, open_blocks(): pl.pallas_call(functools.partial(open_kernel, planes), out_shape=(jax.Sha...  41.9 us
    pallas_call x1, Pallas kernels, chosen_blocks(): pl.pallas_call(chosen_kernel, out_shape=(jax.ShapeDtypeStruct(queries.sha...  5.52 us
    unnamed x2, local copies, waits for them, and re-layouts  4.51 us

profile of v2, /device:TPU:0, one launch (start us, length us, event | category | flops | bytes accessed | tf_op | source)
XLA Modules:
  0.0 104.7 jit_solution(3462054061878230117)
XLA Ops:
  0.0 1.4 %copy.11.selection_ref = s32[16,3]{1,0:T(8,128)} copy(s32[16,3]{0,1:T(4,128)} %param.16) | data formatting | bytes 384 | tf_op args[6]
  1.4 41.9 %open_blocks.1 = (bf16[4,2,2,2,512,128]{5,4,3,2,1,0:T(8,128)(2,1)}, bf16[1024,768]{1,0:T(8,128)(2,1)}, f32[4,128,512]{2,1,0:T(8,128)}, f32[4,512]{1,0:T(4,128)}, bf16[2,2,512,128]{3,2,1,0:T(8,128)(2,1)}) custom-call(bf16[512,128]{1,0:T(8,128)(2,1)} %key_ref.1, bf16[512,128]{1,0:T(8,128)(2,1)} %value_ref.1, bf16[512,512]{1,0:T(8,128)(2,1)} %q_ref.3, ...), custom_call_target="tpu_custom_call" | custom-call | tf_op jit(solution)/shard_map/open_blocks/pallas_call | solution.py:491
  43.2 5.5 %chosen_blocks.1 = (bf16[512,512]{1,0:T(8,128)(2,1)}, bf16[4,2,2,2,512,128]{5,4,3,2,1,0:T(8,128)(2,1)}) custom-call(s32[16,3]{1,0:T(8,128)} %copy.11.selection_ref, bf16[512,512]{1,0:T(8,128)(2,1)} %q_ref.3, bf16[512,512]{1,0:T(8,128)(2,1)} %do_ref.3, f32[4,512]{1,0:T(4,128)} %bitcast.2, f32[4,512]{1,0:T(4,128)} %get-tuple-element.12.delta_ref, ...), custom_call_target="tpu_custom_call" | custom-call | tf_op jit(solution)/shard_map/chosen_blocks/pallas_call | solution.py:558
  48.8 52.8 %close_blocks.1 = bf16[512,2048]{1,0:T(8,128)(2,1)} custom-call(bf16[4,2,2,2,512,128]{5,4,3,2,1,0:T(8,128)(2,1)} %get-tuple-element.16.part_ref, bf16[512,512]{1,0:T(8,128)(2,1)} %get-tuple-element.17.dq_ref, bf16[1024,768]{1,0:T(8,128)(2,1)} %get-tuple-element.18.near_ref, bf16[4096,512]{1,0:T(8,128)(2,1)} %wq_ref.3, bf16[4096,128]{1,0:T(8,128)(2,1)} %wk_ref.3, ...), custom_call_target="tpu_custom_call" | custom-call | tf_op jit(solution)/shard_map/close_blocks/pallas_call | solution.py:730
  101.5 3.2 %copy.13 = bf16[512,2048]{1,0:T(8,128)(2,1)} copy(bf16[512,2048]{1,0:T(8,128)(2,1)} %close_blocks.1) | data formatting | bytes 4194304

commit v3 on v1

--- a/solution.py
+++ b/solution.py
@@ -318,60 +318,391 @@
     )(part)
 
 
+def toward(src, dst, send, recv):
+    return pltpu.make_async_remote_copy(
+        src_ref=src, dst_ref=dst, send_sem=send, recv_sem=recv,
+        device_id={"grp": 1 - lax.axis_index("grp")}, device_id_type=MESH,
+    )
+
+
+def greet_group():
+    pl.semaphore_signal(
+        pltpu.get_barrier_semaphore(), inc=1,
+        device_id={"grp": 1 - lax.axis_index("grp")}, device_id_type=MESH,
+    )
+
+
+def columns(h):
+    return slice(h * HD, (h + 1) * HD)
+
+
+def block_gradients(key, value, q_ref, do_ref, lse_ref, delta_ref, dq_sum, diagonal):
+    heads = q_ref.shape[1] // HD
+    key_t = key.astype(jnp.float32).T.astype(jnp.bfloat16)
+    if diagonal:
+        key_pos = lax.broadcasted_iota(jnp.int32, (BLOCK, BLOCK), 0)
+        query_pos = lax.broadcasted_iota(jnp.int32, (BLOCK, BLOCK), 1)
+        seen = key_pos <= query_pos
+    dk = jnp.zeros((BLOCK, HD), jnp.float32)
+    dv = jnp.zeros((BLOCK, HD), jnp.float32)
+    for h in range(heads):
+        query, cotangent = q_ref[:, columns(h)], do_ref[:, columns(h)]
+        scores = lax.dot_general(key, query, NT, preferred_element_type=jnp.float32)
+        probs = jnp.exp2(scores * (SCALE * LOG2E) - lse_ref[h : h + 1, :] * LOG2E)
+        if diagonal:
+            probs = jnp.where(seen, probs, 0.0)
+        prob_grad = lax.dot_general(value, cotangent, NT, preferred_element_type=jnp.float32)
+        score_half = (probs * (prob_grad - delta_ref[h : h + 1, :])).astype(jnp.bfloat16)
+        probs_half = probs.astype(jnp.bfloat16)
+        dv = dv + lax.dot_general(probs_half, cotangent, NN, preferred_element_type=jnp.float32)
+        dk = dk + lax.dot_general(score_half, query, NN, preferred_element_type=jnp.float32)
+        dq = lax.dot_general(key_t, score_half, NN, preferred_element_type=jnp.float32)
+        dq_sum[h] = dq if diagonal else dq_sum[h] + dq
+    return (dk * SCALE).astype(jnp.bfloat16), dv.astype(jnp.bfloat16)
+
+
 TILE = 256
 
 
-def project_kernel(
-    where_ref, dq_ref, dkv_ref, dq_far_ref, dkv_far_ref, wq_ref, wk_ref, wv_ref, near_ref, far_ref, out_ref
+def fused_kernel(
+    planes, selection_ref, key_ref, value_ref, q_ref, do_ref, o_ref, lse_ref, wq_ref, wk_ref, wv_ref,
+    out_ref,
+    blocks, part, delta, dq_sum, picked, dq, dq_far, mine, theirs, total,
+    c_in, y_in, z_in, y_out, z_out, held, dkv, dkv_far,
+    gz_send, gz_recv, gy_send, gy_recv, gc_send, gc_recv,
+    sz_send, sz_recv, sy_send, sy_recv, sc_send, sc_recv,
+    local_sem, w_send, w_recv, swap_send, swap_recv, x_send, x_recv,
 ):
-    step, half = pl.program_id(0), pl.num_programs(0) // 2
-    feature = dq_ref.shape[1]
+    me, z, y, c = place()
+    group = lax.axis_index("grp")
+    sibling, side = sibling_of(me, c), beside(me, y)
+    heads = q_ref.shape[1] // HD
+    feature = q_ref.shape[1]
+    half = out_ref.shape[1]
+    share = half // 2
+    kinds = range(2)
+
+    greet(sibling)
+    greet(side)
+    greet_group()
+
+    @pl.when(z > 0)
+    def _():
+        greet(me - 4)
+
+    @pl.when(z < planes - 1)
+    def _():
+        greet(me + 4)
+
+    local_rows = pl.ds(pl.multiple_of(group * half, half), half)
+    away_rows = pl.ds(pl.multiple_of((1 - group) * half + c * share, share), share)
+    locals_, weights = [], []
+    first = 0
+    for i, weight in enumerate((wq_ref, wk_ref, wv_ref)):
+        last = first + weight.shape[1]
+        locals_.append(
+            pltpu.make_async_copy(weight.at[local_rows], mine.at[:, first:last], local_sem.at[i])
+        )
+        weights.append(
+            toward(weight.at[away_rows], theirs.at[c, :, first:last], w_send.at[i], w_recv.at[i])
+        )
+        first = last
+    weight_swap = remote(theirs.at[c], theirs.at[c], swap_send, swap_recv, sibling)
+
+    blocks[z, c, 0, y] = key_ref[...]
+    blocks[z, c, 1, y] = value_ref[...]
+    pl.semaphore_wait(
+        pltpu.get_barrier_semaphore(),
+        3 + (z > 0).astype(jnp.int32) + (z < planes - 1).astype(jnp.int32),
+    )
+
+    def up(s, k):
+        slot = blocks.at[z - s, c, k, y]
+        return remote(slot, slot, gz_send.at[s, k], gz_recv.at[s + 1, k], me + 4)
+
+    def from_below(s, k):
+        slot = blocks.at[z - s, c, k, y]
+        return remote(slot, slot, gz_send.at[s, k], gz_recv.at[s, k], me)
+
+    def across(s, k):
+        slot = blocks.at[z - s, c, k, y]
+        return remote(slot, slot, gy_send.at[s, k], gy_recv.at[s, k], side)
+
+    def between(s, k):
+        pair = blocks.at[z - s, c, k]
+        return remote(pair, pair, gc_send.at[s, k], gc_recv.at[s, k], sibling)
+
+    def gradients(key, value, diagonal):
+        return block_gradients(key, value, q_ref, do_ref, lse_ref, delta, dq_sum, diagonal)
+
+    for s in range(planes + 1):
+        for k in kinds:
+            if s < planes:
+
+                @pl.when(z >= s)
+                def _(s=s, k=k):
+                    if s > 0:
+                        from_below(s, k).wait_recv()
+                    if s < planes - 1:
+
+                        @pl.when(z < planes - 1)
+                        def _():
+                            up(s, k).start()
+
+                    across(s, k).start()
+
+            if s > 0:
+
+                @pl.when(z >= s - 1)
+                def _(s=s, k=k):
+                    across(s - 1, k).wait_recv()
+                    between(s - 1, k).start()
+
+        if s == 0:
+            for copy in weights + locals_:
+                copy.start()
+            for h in range(heads):
+                product = do_ref[:, columns(h)].astype(jnp.float32) * o_ref[:, columns(h)].astype(jnp.float32)
+                delta[h : h + 1, :] = jnp.sum(product.T, axis=0, keepdims=True)
+            dk, dv = gradients(key_ref[...], value_ref[...], True)
+            picked[0, 0] = dk
+            picked[0, 1] = dv
+
+        if s == 2:
+            for k in kinds:
+                between(0, k).wait_recv()
+
+                @pl.when(z >= 1)
+                def _(k=k):
+                    between(1, k).wait_recv()
+
+            @pl.when(me > 0)
+            def _():
+                last = me - 1
+                dk, dv = gradients(
+                    blocks[last // 4, last % 2, 0, (last // 2) % 2],
+                    blocks[last // 4, last % 2, 1, (last // 2) % 2],
+                    False,
+                )
+                picked[1, 0] = dk
+                picked[1, 1] = dv
+
+    for s in range(2, planes):
+
+        @pl.when(z >= s)
+        def _(s=s):
+            for k in kinds:
+                between(s, k).wait_recv()
+
+    picks = [selection_ref[me, column] for column in range(TOPK)]
+    others = [
+        jnp.where(picks[0] == me - 1, picks[1], picks[0]),
+        jnp.where(picks[2] == me - 1, picks[1], picks[2]),
+    ]
+    for i, block in enumerate(others):
+        usable = block < me
+        at = jnp.where(usable, block, me)
+        for h in range(heads):
+            dq_sum[heads + h] = dq_sum[h]
+        dk, dv = gradients(
+            blocks[at // 4, at % 2, 0, (at // 2) % 2], blocks[at // 4, at % 2, 1, (at // 2) % 2], False
+        )
+        for h in range(heads):
+            dq_sum[h] = jnp.where(usable, dq_sum[h], dq_sum[heads + h])
+        picked[2 + i, 0] = dk
+        picked[2 + i, 1] = dv
+    for h in range(heads):
+        dq[:, columns(h)] = (dq_sum[h] * SCALE).T.astype(jnp.bfloat16)
+    query_swap = toward(dq, dq_far, x_send.at[2], x_recv.at[2])
+    query_swap.start()
+
+    def inward(t, k):
+        return remote(part.at[t, 1 - c, k], c_in.at[t, k], sc_send.at[t, k], sc_recv.at[t, k], sibling)
+
+    def sideways(t, k):
+        return remote(y_out.at[t, k], y_in.at[t, k], sy_send.at[t, k], sy_recv.at[t, k], side)
+
+    def down(t, k):
+        return remote(z_out.at[t, k], z_in.at[t, k], sz_send.at[t, k], sz_recv.at[t, k], me - 4)
+
+    def keyval_swap(k):
+        return toward(dkv.at[k], dkv_far.at[k], x_send.at[k], x_recv.at[k])
+
+    def place_partials(t, core):
+        for column in range(2):
+            block = t * 4 + column * 2 + core
+            for k in kinds:
+                nothing = jnp.zeros((BLOCK, HD), jnp.bfloat16)
+                chosen = jnp.where((others[0] == block) & (block < me), picked[2, k], nothing)
+                chosen = jnp.where((others[1] == block) & (block < me), picked[3, k], chosen)
+                part[t, core, k, column] = chosen
+
+                @pl.when(block == me)
+                def _(k=k, column=column):
+                    part[t, core, k, column] = picked[0, k]
+
+                @pl.when(block == me - 1)
+                def _(k=k, column=column):
+                    part[t, core, k, column] = picked[1, k]
+
+    for t in range(planes):
+
+        @pl.when(t <= z)
+        def _(t=t):
+            place_partials(t, 1 - c)
+            for k in kinds:
+                inward(t, k).start()
+
+    for t in range(planes):
+
+        @pl.when(t <= z)
+        def _(t=t):
+            place_partials(t, c)
+            for k in kinds:
+                inward(t, k).wait_recv()
+                y_out[t, k] = (
+                    part[t, c, k, 1 - y].astype(jnp.float32) + c_in[t, k, 1 - y].astype(jnp.float32)
+                ).astype(jnp.bfloat16)
+                sideways(t, k).start()
+                held[t, k] = part[t, c, k, y].astype(jnp.float32) + c_in[t, k, y].astype(jnp.float32)
 
     def dot(lhs, rhs):
         return lax.dot_general(lhs, rhs, NT, preferred_element_type=jnp.float32)
 
-    total = dot(dq_ref[...], wq_ref[...])
-    total += dot(dkv_ref[:, :HD], wk_ref[...])
-    total += dot(dkv_ref[:, HD:], wv_ref[...])
-    weights = jnp.where(step < half, near_ref[...], far_ref[...])
-    total += dot(dq_far_ref[...], weights[:, :feature])
-    total += dot(dkv_far_ref[...], weights[:, feature:])
-    out_ref[...] = total.astype(jnp.bfloat16)
-
-
-def project(dq, dkv, dq_far, dkv_far, wq, wk, wv, near, far):
-    rows = dq.shape[0]
-    half = near.shape[0] // TILE
-    where = jnp.stack([lax.axis_index("grp"), lax.axis_index("ctx") % 2]).astype(jnp.int32)
-
-    def column(i, where):
-        core = jnp.where(i < half, where[1], 1 - where[1])
-        return core * half + i % half
-
-    def whole(array):
-        return pl.BlockSpec(array.shape, lambda i, where: (0, 0))
-
-    def mine(array):
-        return pl.BlockSpec(
-            (TILE, array.shape[1]), lambda i, where: (where[0] * 2 * half + column(i, where), 0)
+    def tiles(body):
+        @pl.loop(0, half // TILE)
+        def _(j):
+            here = pl.ds(pl.multiple_of(j * TILE, TILE), TILE)
+            there = (j * TILE // share, pl.ds(pl.multiple_of(j * TILE % share, TILE), TILE))
+            body(here, there)
+
+    for copy in locals_:
+        copy.wait()
+
+    def project_query(here, there):
+        total[:, here] = dot(dq[...], mine[here, :feature])
+
+    tiles(project_query)
+    for copy in weights:
+        copy.wait_recv()
+    weight_swap.start()
+
+    def project_query_far(here, there):
+        total[:, here] += dot(dq_far[...], theirs[there[0], there[1], :feature])
+
+    for t in range(planes):
+
+        @pl.when(t <= z)
+        def _(t=t):
+            @pl.when(t == z)
+            def _():
+                query_swap.wait()
+                weight_swap.wait()
+                tiles(project_query_far)
+
+            for k in kinds:
+                sideways(t, k).wait_recv()
+                held[t, k] += y_in[t, k].astype(jnp.float32)
+
+                @pl.when(z < planes - 1)
+                def _(k=k):
+                    down(t, k).wait_recv()
+                    held[t, k] += z_in[t, k].astype(jnp.float32)
+
+                @pl.when(t < z)
+                def _(k=k):
+                    z_out[t, k] = held[t, k].astype(jnp.bfloat16)
+                    down(t, k).start()
+
+                @pl.when(t == z)
+                def _(k=k):
+                    dkv[k] = held[t, k].astype(jnp.bfloat16)
+                    keyval_swap(k).start()
+
+    def project_keyval(here, there):
+        total[:, here] += dot(dkv[0], mine[here, feature : feature + HD]) + dot(
+            dkv[1], mine[here, feature + HD :]
         )
 
+    tiles(project_keyval)
+    for s in range(planes):
+
+        @pl.when(z >= s)
+        def _(s=s):
+            for k in kinds:
+                if s < planes - 1:
+
+                    @pl.when(z < planes - 1)
+                    def _(k=k):
+                        up(s, k).wait_send()
+
+                across(s, k).wait_send()
+                between(s, k).wait_send()
+                inward(s, k).wait_send()
+                sideways(s, k).wait_send()
+
+                @pl.when(s < z)
+                def _(k=k):
+                    down(s, k).wait_send()
+
+    for copy in weights:
+        copy.wait_send()
+    for k in kinds:
+        keyval_swap(k).wait()
+
+    def project_keyval_far(here, there):
+        out_ref[:, here] = (
+            total[:, here]
+            + dot(dkv_far[0], theirs[there[0], there[1], feature : feature + HD])
+            + dot(dkv_far[1], theirs[there[0], there[1], feature + HD :])
+        ).astype(jnp.bfloat16)
+
+    tiles(project_keyval_far)
+
+
+def fused(selection, key, value, queries, output_grad, output_rows, lse, weights, planes):
+    rows, width = queries.shape
+    heads = width // HD
+    half = weights[0].shape[0] // 2
+    features = sum(weight.shape[1] for weight in weights)
+    dma = pltpu.SemaphoreType.DMA
+    vmem = pl.BlockSpec(memory_space=pltpu.VMEM)
+    anywhere = pl.BlockSpec(memory_space=pl.ANY)
+
+    def half_type(*shape):
+        return pltpu.VMEM(shape, jnp.bfloat16)
+
+    def full_type(*shape):
+        return pltpu.VMEM(shape, jnp.float32)
+
+    slots = half_type(planes, 2, rows, HD)
     return pl.pallas_call(
-        project_kernel,
-        out_shape=jax.ShapeDtypeStruct((rows, 2 * half * TILE), jnp.bfloat16),
-        grid_spec=pltpu.PrefetchScalarGridSpec(
-            num_scalar_prefetch=1,
-            grid=(2 * half,),
-            in_specs=[
-                whole(dq), whole(dkv), whole(dq_far), whole(dkv_far), mine(wq), mine(wk), mine(wv),
-                pl.BlockSpec((TILE, near.shape[1]), lambda i, where: (jnp.minimum(i, half - 1), 0)),
-                pl.BlockSpec((TILE, near.shape[1]), lambda i, where: (jnp.maximum(i - half, 0), 0)),
-            ],
-            out_specs=pl.BlockSpec((rows, TILE), lambda i, where: (0, column(i, where))),
+        functools.partial(fused_kernel, planes),
+        out_shape=jax.ShapeDtypeStruct((rows, half), jnp.bfloat16),
+        in_specs=[pl.BlockSpec(memory_space=pltpu.SMEM)] + [vmem] * 6 + [anywhere] * 3,
+        out_specs=vmem,
+        scratch_shapes=[
+            half_type(planes, 2, 2, 2, rows, HD),
+            half_type(planes, 2, 2, 2, rows, HD),
+            full_type(heads, rows),
+            full_type(2 * heads, HD, rows),
+            half_type(4, 2, rows, HD),
+            half_type(rows, width),
+            half_type(rows, width),
+            half_type(half, features),
+            half_type(2, half // 2, features),
+            full_type(rows, half),
+            half_type(planes, 2, 2, rows, HD),
+            slots, slots, slots, slots,
+            full_type(planes, 2, rows, HD),
+            half_type(2, rows, HD),
+            half_type(2, rows, HD),
+        ] + [dma((planes, 2))] * 12 + [dma((3,)), dma((3,)), dma((3,)), dma(()), dma(()), dma((3,)), dma((3,))],
+        compiler_params=pltpu.CompilerParams(
+            collective_id=2, has_side_effects=True, vmem_limit_bytes=VMEM_LIMIT
         ),
-        compiler_params=pltpu.CompilerParams(vmem_limit_bytes=VMEM_LIMIT),
-        name="project",
-    )(where, dq, dkv, dq_far, dkv_far, wq, wk, wv, near, far)
+        name="fused",
+    )(selection, key, value, queries, output_grad, output_rows, lse, *weights)
 
 
 def on_device(
@@ -382,23 +713,12 @@
     contexts = lax.axis_size("ctx")
     groups = lax.axis_size("grp")
     planes = contexts // 4
-    paired = groups == 2
-
-    if paired:
-        group, core = lax.axis_index("grp"), position % 2
-        share = query_weight.shape[0] // 4
-        start = (1 - group) * 2 * share + core * share
-        swap = [(0, 1), (1, 0)]
-        siblings = [(i, i ^ 1) for i in range(contexts)]
-        outgoing = jnp.concatenate(
-            [
-                lax.dynamic_slice_in_dim(weight, start, share, 0)
-                for weight in (query_weight, key_weight, value_weight)
-            ],
-            axis=1,
+    if groups == 2:
+        weights = (query_weight, key_weight, value_weight)
+        lse = log_normalizer.T
+        return fused(
+            selection, key_rows, value_rows, queries, output_grad, output_rows, lse, weights, planes
         )
-        near = lax.ppermute(outgoing, "grp", swap)
-        far = lax.ppermute(near, "ctx", siblings)
 
     blocks = gather_blocks(jnp.concatenate([key_rows, value_rows], axis=1), planes)
     row = lax.dynamic_index_in_dim(selection, position, 0, keepdims=False).astype(jnp.int32)
@@ -407,15 +727,7 @@
     grad_query, part = attend(
         chosen, usable, queries, output_grad, output_rows, log_normalizer.T, blocks
     )
-    if paired:
-        query_far = lax.ppermute(grad_query, "grp", swap)
     grad_keyval = scatter_blocks(part, planes)
-    if paired:
-        keyval_far = lax.ppermute(grad_keyval, "grp", swap)
-        return project(
-            grad_query, grad_keyval, query_far, keyval_far,
-            query_weight, key_weight, value_weight, near, far,
-        )
     dot = functools.partial(lax.dot_general, dimension_numbers=NT, preferred_element_type=jnp.float32)
     combined = dot(grad_query, query_weight)
     combined = combined + dot(grad_keyval[:, :HD], key_weight)

time: 150 us -> 75.6 us (0.50)
  waiting for transfers between devices: 40.1 us -> 0 us
  Pallas kernels: 97 us -> 70.9 us
  starting transfers between devices: 5.11 us -> 0 us
  other arithmetic: 2.77 us -> 0 us
    ppermute x4 -> x0, waiting for transfers between devices: 40.1 us -> none  [the longest x1 34.4 us: on_device(): near = lax.ppermute(outgoing, 'grp', swap)]
    pallas_call x4 -> x1, Pallas kernels: 97 us -> 70.9 us  [fused(): pl.pallas_call(functools.partial(fused_kernel, planes), out_shape=jax.Sha...]
    ppermute x4 -> x0, starting transfers between devices: 5.11 us -> none  [the longest x1 3.01 us: on_device(): near = lax.ppermute(outgoing, 'grp', swap)]
    dynamic_slice x3 -> x0, local copies, waits for them, and re-layouts: 2.6 us -> none  [the longest x2 2.41 us: on_device(): lax.dynamic_slice_in_dim(weight, start, share, 0)]
    unnamed x14 -> x2, local copies, waits for them, and re-layouts: 2.03 us -> 4.51 us
    concatenate x4 -> x0, other arithmetic: 2.17 us -> none  [the longest x1 0.84 us: on_device(): jnp.concatenate([key_rows, value_rows], axis=1)]
  transfers between devices with their start and end apart: 4 -> 0, of which waited for: 2 -> 0; matrix products, arithmetic and copies ran while one was open for 2% -> 0% of each run, Pallas kernels for 58% -> 0%
where the time goes in v3:
time: 75.6 us; the launch traced here: 75.4 us
  Pallas kernels  70.9 us (94%)
  local copies, waits for them, and re-layouts  4.51 us (6%)
    pallas_call x1, Pallas kernels, fused(): pl.pallas_call(functools.partial(fused_kernel, planes), out_shape=jax.Sha...  70.9 us
    unnamed x2, local copies, waits for them, and re-layouts  4.51 us

profile of v3, /device:TPU:0, one launch (start us, length us, event | category | flops | bytes accessed | tf_op | source)
XLA Modules:
  0.0 75.4 jit_solution(13247503048359162516)
XLA Ops:
  0.0 1.4 %copy.11.selection_ref = s32[16,3]{1,0:T(8,128)} copy(s32[16,3]{0,1:T(4,128)} %param.16) | data formatting | bytes 384 | tf_op args[6]
  1.4 70.9 %fused.1 = bf16[512,2048]{1,0:T(8,128)(2,1)} custom-call(s32[16,3]{1,0:T(8,128)} %copy.11.selection_ref, bf16[512,128]{1,0:T(8,128)(2,1)} %key_ref.1, bf16[512,128]{1,0:T(8,128)(2,1)} %value_ref.1, bf16[512,512]{1,0:T(8,128)(2,1)} %q_ref.1, bf16[512,512]{1,0:T(8,128)(2,1)} %do_ref.1, bf16[512,512]{1,0:T(8,128)(2,1)} %o_ref.1, f32[4,512]{1,0:T(4,128)} %bitcast.1, ...), custom_call_target="tpu_custom_call" | custom-call | tf_op jit(solution)/shard_map/fused/pallas_call | solution.py:679
  72.3 3.2 %copy.13 = bf16[512,2048]{1,0:T(8,128)(2,1)} copy(bf16[512,2048]{1,0:T(8,128)(2,1)} %fused.1) | data formatting | bytes 4194304

commit v4 on v3

--- a/solution.py
+++ b/solution.py
@@ -366,12 +366,13 @@
 
 def fused_kernel(
     planes, selection_ref, key_ref, value_ref, q_ref, do_ref, o_ref, lse_ref, wq_ref, wk_ref, wv_ref,
-    out_ref,
+    out_ref, dkv_far, far_ref,
     blocks, part, delta, dq_sum, picked, dq, dq_far, mine, theirs, total,
-    c_in, y_in, z_in, y_out, z_out, held, dkv, dkv_far,
+    c_in, y_in, z_in, y_out, z_out, held, dkv, summed, extra_in,
     gz_send, gz_recv, gy_send, gy_recv, gc_send, gc_recv,
     sz_send, sz_recv, sy_send, sy_recv, sc_send, sc_recv,
     local_sem, w_send, w_recv, swap_send, swap_recv, x_send, x_recv,
+    extra_send, extra_recv, write_sem,
 ):
     me, z, y, c = place()
     group = lax.axis_index("grp")
@@ -432,6 +433,10 @@
         pair = blocks.at[z - s, c, k]
         return remote(pair, pair, gc_send.at[s, k], gc_recv.at[s, k], sibling)
 
+    def extra_up():
+        slot = blocks.at[0, c, 1, 1 - y]
+        return remote(slot, slot, extra_send.at[0], extra_recv.at[0], me + 4)
+
     def gradients(key, value, diagonal):
         return block_gradients(key, value, q_ref, do_ref, lse_ref, delta, dq_sum, diagonal)
 
@@ -449,13 +454,23 @@
                         def _():
                             up(s, k).start()
 
-                    across(s, k).start()
+                    if (s, k) != (planes - 1, 1):
+                        across(s, k).start()
 
             if s > 0:
 
                 @pl.when(z >= s - 1)
                 def _(s=s, k=k):
-                    across(s - 1, k).wait_recv()
+                    if (s, k) != (planes, 1):
+                        across(s - 1, k).wait_recv()
+                    else:
+                        extra_up().wait_recv()
+                    if (s, k) == (planes - 1, 1):
+
+                        @pl.when(z == planes - 2)
+                        def _():
+                            extra_up().start()
+
                     between(s - 1, k).start()
 
         if s == 0:
@@ -494,7 +509,7 @@
             for k in kinds:
                 between(s, k).wait_recv()
 
-    picks = [selection_ref[me, column] for column in range(TOPK)]
+    picks = [selection_ref[column, me] for column in range(TOPK)]
     others = [
         jnp.where(picks[0] == me - 1, picks[1], picks[0]),
         jnp.where(picks[2] == me - 1, picks[1], picks[2]),
@@ -525,6 +540,9 @@
     def down(t, k):
         return remote(z_out.at[t, k], z_in.at[t, k], sz_send.at[t, k], sz_recv.at[t, k], me - 4)
 
+    def extra_down():
+        return remote(y_out.at[0, 0], extra_in, extra_send.at[1], extra_recv.at[1], me - 4)
+
     def keyval_swap(k):
         return toward(dkv.at[k], dkv_far.at[k], x_send.at[k], x_recv.at[k])
 
@@ -558,13 +576,32 @@
         @pl.when(t <= z)
         def _(t=t):
             place_partials(t, c)
-            for k in kinds:
+            for k in (1, 0) if t == 0 else (0, 1):
                 inward(t, k).wait_recv()
-                y_out[t, k] = (
-                    part[t, c, k, 1 - y].astype(jnp.float32) + c_in[t, k, 1 - y].astype(jnp.float32)
-                ).astype(jnp.bfloat16)
-                sideways(t, k).start()
+                away = part[t, c, k, 1 - y].astype(jnp.float32) + c_in[t, k, 1 - y].astype(jnp.float32)
                 held[t, k] = part[t, c, k, y].astype(jnp.float32) + c_in[t, k, y].astype(jnp.float32)
+                if (t, k) != (0, 0):
+                    y_out[t, k] = away.astype(jnp.bfloat16)
+                    sideways(t, k).start()
+                else:
+
+                    @pl.when(z == planes - 1)
+                    def _():
+                        y_out[t, k] = away.astype(jnp.bfloat16)
+                        extra_down().start()
+                        z_out[t, k] = held[t, k].astype(jnp.bfloat16)
+                        down(t, k).start()
+
+                    @pl.when(z == planes - 2)
+                    def _():
+                        extra_down().wait_recv()
+                        y_out[t, k] = (away + extra_in[...].astype(jnp.float32)).astype(jnp.bfloat16)
+                        sideways(t, k).start()
+
+                    @pl.when(z < planes - 2)
+                    def _():
+                        y_out[t, k] = away.astype(jnp.bfloat16)
+                        sideways(t, k).start()
 
     def dot(lhs, rhs):
         return lax.dot_general(lhs, rhs, NT, preferred_element_type=jnp.float32)
@@ -601,15 +638,18 @@
                 tiles(project_query_far)
 
             for k in kinds:
-                sideways(t, k).wait_recv()
-                held[t, k] += y_in[t, k].astype(jnp.float32)
+
+                @pl.when((z < planes - 1) | ((t, k) != (0, 0)))
+                def _(k=k):
+                    sideways(t, k).wait_recv()
+                    held[t, k] += y_in[t, k].astype(jnp.float32)
 
                 @pl.when(z < planes - 1)
                 def _(k=k):
                     down(t, k).wait_recv()
                     held[t, k] += z_in[t, k].astype(jnp.float32)
 
-                @pl.when(t < z)
+                @pl.when((t < z) & ((z < planes - 1) | ((t, k) != (0, 0))))
                 def _(k=k):
                     z_out[t, k] = held[t, k].astype(jnp.bfloat16)
                     down(t, k).start()
@@ -620,11 +660,19 @@
                     keyval_swap(k).start()
 
     def project_keyval(here, there):
-        total[:, here] += dot(dkv[0], mine[here, feature : feature + HD]) + dot(
-            dkv[1], mine[here, feature + HD :]
-        )
+        summed[:, here] = (
+            total[:, here]
+            + dot(dkv[0], mine[here, feature : feature + HD])
+            + dot(dkv[1], mine[here, feature + HD :])
+        ).astype(jnp.bfloat16)
 
     tiles(project_keyval)
+    written = [
+        pltpu.make_async_copy(summed, out_ref, write_sem.at[0]),
+        pltpu.make_async_copy(theirs.at[:, :, feature:], far_ref, write_sem.at[1]),
+    ]
+    for copy in written:
+        copy.start()
     for s in range(planes):
 
         @pl.when(z >= s)
@@ -636,28 +684,59 @@
                     def _(k=k):
                         up(s, k).wait_send()
 
-                across(s, k).wait_send()
+                if (s, k) != (planes - 1, 1):
+                    across(s, k).wait_send()
                 between(s, k).wait_send()
                 inward(s, k).wait_send()
-                sideways(s, k).wait_send()
+
+                @pl.when((z < planes - 1) | ((s, k) != (0, 0)))
+                def _(k=k):
+                    sideways(s, k).wait_send()
 
                 @pl.when(s < z)
                 def _(k=k):
                     down(s, k).wait_send()
+
+    @pl.when(z == planes - 2)
+    def _():
+        extra_up().wait_send()
+
+    @pl.when(z == planes - 1)
+    def _():
+        extra_down().wait_send()
 
     for copy in weights:
         copy.wait_send()
     for k in kinds:
         keyval_swap(k).wait()
-
-    def project_keyval_far(here, there):
-        out_ref[:, here] = (
-            total[:, here]
-            + dot(dkv_far[0], theirs[there[0], there[1], feature : feature + HD])
-            + dot(dkv_far[1], theirs[there[0], there[1], feature + HD :])
-        ).astype(jnp.bfloat16)
-
-    tiles(project_keyval_far)
+    for copy in written:
+        copy.wait()
+
+
+def finish_kernel(summed_ref, dkv_ref, far_ref, out_ref):
+    out_ref[...] = (
+        summed_ref[...].astype(jnp.float32)
+        + lax.dot_general(dkv_ref[0], far_ref[:, :HD], NT, preferred_element_type=jnp.float32)
+        + lax.dot_general(dkv_ref[1], far_ref[:, HD:], NT, preferred_element_type=jnp.float32)
+    ).astype(jnp.bfloat16)
+
+
+def finish(summed, dkv_far, far):
+    rows, half = summed.shape
+    wide = 2 * TILE
+    column = pl.BlockSpec((rows, wide), lambda j: (0, j))
+    return pl.pallas_call(
+        finish_kernel,
+        out_shape=jax.ShapeDtypeStruct(summed.shape, jnp.bfloat16),
+        grid=(half // wide,),
+        in_specs=[
+            column,
+            pl.BlockSpec(dkv_far.shape, lambda j: (0, 0, 0)),
+            pl.BlockSpec((wide, far.shape[1]), lambda j: (j, 0)),
+        ],
+        out_specs=column,
+        name="finish",
+    )(summed, dkv_far, far)
 
 
 def fused(selection, key, value, queries, output_grad, output_rows, lse, weights, planes):
@@ -676,11 +755,15 @@
         return pltpu.VMEM(shape, jnp.float32)
 
     slots = half_type(planes, 2, rows, HD)
-    return pl.pallas_call(
+    summed, dkv_far, far = pl.pallas_call(
         functools.partial(fused_kernel, planes),
-        out_shape=jax.ShapeDtypeStruct((rows, half), jnp.bfloat16),
+        out_shape=(
+            jax.ShapeDtypeStruct((rows, half), jnp.bfloat16),
+            jax.ShapeDtypeStruct((2, rows, HD), jnp.bfloat16),
+            jax.ShapeDtypeStruct((2, half // 2, 2 * HD), jnp.bfloat16),
+        ),
         in_specs=[pl.BlockSpec(memory_space=pltpu.SMEM)] + [vmem] * 6 + [anywhere] * 3,
-        out_specs=vmem,
+        out_specs=(anywhere,) * 3,
         scratch_shapes=[
             half_type(planes, 2, 2, 2, rows, HD),
             half_type(planes, 2, 2, 2, rows, HD),
@@ -696,13 +779,15 @@
             slots, slots, slots, slots,
             full_type(planes, 2, rows, HD),
             half_type(2, rows, HD),
-            half_type(2, rows, HD),
-        ] + [dma((planes, 2))] * 12 + [dma((3,)), dma((3,)), dma((3,)), dma(()), dma(()), dma((3,)), dma((3,))],
+            half_type(rows, half),
+            half_type(rows, HD),
+        ] + [dma((planes, 2))] * 12 + [dma((3,)), dma((3,)), dma((3,)), dma(()), dma(()), dma((3,)), dma((3,)), dma((2,)), dma((2,)), dma((2,))],
         compiler_params=pltpu.CompilerParams(
             collective_id=2, has_side_effects=True, vmem_limit_bytes=VMEM_LIMIT
         ),
         name="fused",
     )(selection, key, value, queries, output_grad, output_rows, lse, *weights)
+    return finish(summed, dkv_far, far.reshape(half, 2 * HD))
 
 
 def on_device(
@@ -717,7 +802,7 @@
         weights = (query_weight, key_weight, value_weight)
         lse = log_normalizer.T
         return fused(
-            selection, key_rows, value_rows, queries, output_grad, output_rows, lse, weights, planes
+            selection.T, key_rows, value_rows, queries, output_grad, output_rows, lse, weights, planes
         )
 
     blocks = gather_blocks(jnp.concatenate([key_rows, value_rows], axis=1), planes)

time: 75.6 us -> 70.5 us (0.933)
  local copies, waits for them, and re-layouts: 4.51 us -> 0 us
    unnamed x2 -> x0, local copies, waits for them, and re-layouts: 4.51 us -> none
    pallas_call x1 -> x2, Pallas kernels: 70.9 us -> 70.2 us  [the longest x1 65.4 us: fused(): pl.pallas_call(functools.partial(fused_kernel, planes), out_shape=(jax.Sh...]
where the time goes in v4:
time: 70.5 us; the launch traced here: 70.3 us
  Pallas kernels  70.2 us (100%)
    pallas_call x1, Pallas kernels, fused(): pl.pallas_call(functools.partial(fused_kernel, planes), out_shape=(jax.Sh...  65.4 us
    pallas_call x1, Pallas kernels, finish(): pl.pallas_call(finish_kernel, out_shape=jax.ShapeDtypeStruct(summed.shape...  4.84 us

profile of v4, /device:TPU:0, one launch (start us, length us, event | category | flops | bytes accessed | tf_op | source)
XLA Modules:
  0.0 70.3 jit_solution(10742534140117113242)
XLA Ops:
  0.0 65.4 %fused.1 = (bf16[512,2048]{1,0:T(8,128)(2,1)}, bf16[2,512,128]{2,1,0:T(8,128)(2,1)}, bf16[2,1024,256]{2,1,0:T(8,128)(2,1)}) custom-call(s32[3,16]{1,0:T(4,128)} %bitcast.5, bf16[512,128]{1,0:T(8,128)(2,1)} %key_ref.1, bf16[512,128]{1,0:T(8,128)(2,1)} %value_ref.1, bf16[512,512]{1,0:T(8,128)(2,1)} %q_ref.1, bf16[512,512]{1,0:T(8,128)(2,1)} %do_ref.1, ...), custom_call_target="tpu_custom_call" | custom-call | tf_op jit(solution)/shard_map/fused/pallas_call | solution.py:758
  65.4 4.8 %finish.1 = bf16[512,2048]{1,0:T(8,128)(2,1)} custom-call(bf16[512,2048]{1,0:T(8,128)(2,1)} %get-tuple-element.8.summed_ref, bf16[2,512,128]{2,1,0:T(8,128)(2,1)} %get-tuple-element.9.dkv_ref, bf16[2048,256]{1,0:T(8,128)(2,1)} %bitcast.3), custom_call_target="tpu_custom_call" | custom-call | tf_op jit(solution)/shard_map/finish/pallas_call | solution.py:728

commit v5 on v4

--- a/solution.py
+++ b/solution.py
@@ -336,20 +336,21 @@
     return slice(h * HD, (h + 1) * HD)
 
 
-def block_gradients(key, value, q_ref, do_ref, lse_ref, delta_ref, dq_sum, diagonal):
+def part_gradients(key, value, q_ref, do_ref, lse_ref, delta_ref, dq_sum, diagonal=None, usable=None):
     heads = q_ref.shape[1] // HD
+    count, rows = key.shape[0], q_ref.shape[0]
     key_t = key.astype(jnp.float32).T.astype(jnp.bfloat16)
-    if diagonal:
-        key_pos = lax.broadcasted_iota(jnp.int32, (BLOCK, BLOCK), 0)
-        query_pos = lax.broadcasted_iota(jnp.int32, (BLOCK, BLOCK), 1)
+    if diagonal is not None:
+        key_pos = lax.broadcasted_iota(jnp.int32, (count, rows), 0) + diagonal
+        query_pos = lax.broadcasted_iota(jnp.int32, (count, rows), 1)
         seen = key_pos <= query_pos
-    dk = jnp.zeros((BLOCK, HD), jnp.float32)
-    dv = jnp.zeros((BLOCK, HD), jnp.float32)
+    dk = jnp.zeros((count, HD), jnp.float32)
+    dv = jnp.zeros((count, HD), jnp.float32)
     for h in range(heads):
         query, cotangent = q_ref[:, columns(h)], do_ref[:, columns(h)]
         scores = lax.dot_general(key, query, NT, preferred_element_type=jnp.float32)
         probs = jnp.exp2(scores * (SCALE * LOG2E) - lse_ref[h : h + 1, :] * LOG2E)
-        if diagonal:
+        if diagonal is not None:
             probs = jnp.where(seen, probs, 0.0)
         prob_grad = lax.dot_general(value, cotangent, NT, preferred_element_type=jnp.float32)
         score_half = (probs * (prob_grad - delta_ref[h : h + 1, :])).astype(jnp.bfloat16)
@@ -357,7 +358,9 @@
         dv = dv + lax.dot_general(probs_half, cotangent, NN, preferred_element_type=jnp.float32)
         dk = dk + lax.dot_general(score_half, query, NN, preferred_element_type=jnp.float32)
         dq = lax.dot_general(key_t, score_half, NN, preferred_element_type=jnp.float32)
-        dq_sum[h] = dq if diagonal else dq_sum[h] + dq
+        if usable is not None:
+            dq = jnp.where(usable, dq, 0.0)
+        dq_sum[h] = dq if diagonal == 0 else dq_sum[h] + dq
     return (dk * SCALE).astype(jnp.bfloat16), dv.astype(jnp.bfloat16)
 
 
@@ -381,7 +384,10 @@
     feature = q_ref.shape[1]
     half = out_ref.shape[1]
     share = half // 2
-    kinds = range(2)
+    piece = q_ref.shape[0] // 2
+    pieces = range(4)
+    early = (0, 1)
+    late = (2, 3)
 
     greet(sibling)
     greet(side)
@@ -410,8 +416,9 @@
         first = last
     weight_swap = remote(theirs.at[c], theirs.at[c], swap_send, swap_recv, sibling)
 
-    blocks[z, c, 0, y] = key_ref[...]
-    blocks[z, c, 1, y] = value_ref[...]
+    for r in range(2):
+        blocks[z, c, 2 * r, y] = key_ref[r * piece : (r + 1) * piece, :]
+        blocks[z, c, 2 * r + 1, y] = value_ref[r * piece : (r + 1) * piece, :]
     pl.semaphore_wait(
         pltpu.get_barrier_semaphore(),
         3 + (z > 0).astype(jnp.int32) + (z < planes - 1).astype(jnp.int32),
@@ -433,15 +440,20 @@
         pair = blocks.at[z - s, c, k]
         return remote(pair, pair, gc_send.at[s, k], gc_recv.at[s, k], sibling)
 
-    def extra_up():
-        slot = blocks.at[0, c, 1, 1 - y]
-        return remote(slot, slot, extra_send.at[0], extra_recv.at[0], me + 4)
-
-    def gradients(key, value, diagonal):
-        return block_gradients(key, value, q_ref, do_ref, lse_ref, delta, dq_sum, diagonal)
+    def extra_up(k):
+        slot = blocks.at[0, c, k, 1 - y]
+        return remote(slot, slot, extra_send.at[k], extra_recv.at[k], me + 4)
+
+    def gradients(key, value, **kind):
+        return part_gradients(key, value, q_ref, do_ref, lse_ref, delta, dq_sum, **kind)
+
+    def stored(block, r):
+        at = (block // 4, block % 2)
+        column = ((block // 2) % 2,)
+        return blocks[at + (2 * r,) + column], blocks[at + (2 * r + 1,) + column]
 
     for s in range(planes + 1):
-        for k in kinds:
+        for k in pieces:
             if s < planes:
 
                 @pl.when(z >= s)
@@ -454,22 +466,22 @@
                         def _():
                             up(s, k).start()
 
-                    if (s, k) != (planes - 1, 1):
+                    if s < planes - 1 or k in early:
                         across(s, k).start()
 
             if s > 0:
 
                 @pl.when(z >= s - 1)
                 def _(s=s, k=k):
-                    if (s, k) != (planes, 1):
+                    if s < planes or k in early:
                         across(s - 1, k).wait_recv()
                     else:
-                        extra_up().wait_recv()
-                    if (s, k) == (planes - 1, 1):
+                        extra_up(k).wait_recv()
+                    if s == planes - 1 and k in late:
 
                         @pl.when(z == planes - 2)
                         def _():
-                            extra_up().start()
+                            extra_up(k).start()
 
                     between(s - 1, k).start()
 
@@ -479,12 +491,14 @@
             for h in range(heads):
                 product = do_ref[:, columns(h)].astype(jnp.float32) * o_ref[:, columns(h)].astype(jnp.float32)
                 delta[h : h + 1, :] = jnp.sum(product.T, axis=0, keepdims=True)
-            dk, dv = gradients(key_ref[...], value_ref[...], True)
-            picked[0, 0] = dk
-            picked[0, 1] = dv
+            for r in range(2):
+                rows = slice(r * piece, (r + 1) * piece)
+                dk, dv = gradients(key_ref[rows, :], value_ref[rows, :], diagonal=r * piece)
+                picked[0, 2 * r] = dk
+                picked[0, 2 * r + 1] = dv
 
         if s == 2:
-            for k in kinds:
+            for k in pieces:
                 between(0, k).wait_recv()
 
                 @pl.when(z >= 1)
@@ -493,20 +507,16 @@
 
             @pl.when(me > 0)
             def _():
-                last = me - 1
-                dk, dv = gradients(
-                    blocks[last // 4, last % 2, 0, (last // 2) % 2],
-                    blocks[last // 4, last % 2, 1, (last // 2) % 2],
-                    False,
-                )
-                picked[1, 0] = dk
-                picked[1, 1] = dv
+                for r in range(2):
+                    dk, dv = gradients(*stored(me - 1, r))
+                    picked[1, 2 * r] = dk
+                    picked[1, 2 * r + 1] = dv
 
     for s in range(2, planes):
 
         @pl.when(z >= s)
         def _(s=s):
-            for k in kinds:
+            for k in pieces:
                 between(s, k).wait_recv()
 
     picks = [selection_ref[column, me] for column in range(TOPK)]
@@ -514,25 +524,19 @@
         jnp.where(picks[0] == me - 1, picks[1], picks[0]),
         jnp.where(picks[2] == me - 1, picks[1], picks[2]),
     ]
-    for i, block in enumerate(others):
-        usable = block < me
-        at = jnp.where(usable, block, me)
-        for h in range(heads):
-            dq_sum[heads + h] = dq_sum[h]
-        dk, dv = gradients(
-            blocks[at // 4, at % 2, 0, (at // 2) % 2], blocks[at // 4, at % 2, 1, (at // 2) % 2], False
+
+    def chosen_gradients(i, r):
+        usable = others[i] < me
+        key, value = stored(jnp.where(usable, others[i], me), r)
+        dk, dv = gradients(key, value, usable=usable)
+        picked[2 + i, 2 * r] = dk
+        picked[2 + i, 2 * r + 1] = dv
+
+    def inward(t, r):
+        pair = pl.ds(2 * r, 2)
+        return remote(
+            part.at[t, 1 - c, pair], c_in.at[t, pair], sc_send.at[t, r], sc_recv.at[t, r], sibling
         )
-        for h in range(heads):
-            dq_sum[h] = jnp.where(usable, dq_sum[h], dq_sum[heads + h])
-        picked[2 + i, 0] = dk
-        picked[2 + i, 1] = dv
-    for h in range(heads):
-        dq[:, columns(h)] = (dq_sum[h] * SCALE).T.astype(jnp.bfloat16)
-    query_swap = toward(dq, dq_far, x_send.at[2], x_recv.at[2])
-    query_swap.start()
-
-    def inward(t, k):
-        return remote(part.at[t, 1 - c, k], c_in.at[t, k], sc_send.at[t, k], sc_recv.at[t, k], sibling)
 
     def sideways(t, k):
         return remote(y_out.at[t, k], y_in.at[t, k], sy_send.at[t, k], sy_recv.at[t, k], side)
@@ -540,17 +544,20 @@
     def down(t, k):
         return remote(z_out.at[t, k], z_in.at[t, k], sz_send.at[t, k], sz_recv.at[t, k], me - 4)
 
-    def extra_down():
-        return remote(y_out.at[0, 0], extra_in, extra_send.at[1], extra_recv.at[1], me - 4)
+    def extra_down(k):
+        return remote(y_out.at[0, k], extra_in.at[k], extra_send.at[k], extra_recv.at[2 + k], me - 4)
+
+    def spot(k):
+        return slice(k // 2 * piece, (k // 2 + 1) * piece), slice(k % 2 * HD, (k % 2 + 1) * HD)
 
     def keyval_swap(k):
-        return toward(dkv.at[k], dkv_far.at[k], x_send.at[k], x_recv.at[k])
-
-    def place_partials(t, core):
+        return toward(dkv.at[spot(k)], dkv_far.at[spot(k)], x_send.at[k], x_recv.at[k])
+
+    def place_partials(t, core, r):
         for column in range(2):
             block = t * 4 + column * 2 + core
-            for k in kinds:
-                nothing = jnp.zeros((BLOCK, HD), jnp.bfloat16)
+            for k in (2 * r, 2 * r + 1):
+                nothing = jnp.zeros((piece, HD), jnp.bfloat16)
                 chosen = jnp.where((others[0] == block) & (block < me), picked[2, k], nothing)
                 chosen = jnp.where((others[1] == block) & (block < me), picked[3, k], chosen)
                 part[t, core, k, column] = chosen
@@ -563,45 +570,66 @@
                 def _(k=k, column=column):
                     part[t, core, k, column] = picked[1, k]
 
-    for t in range(planes):
-
+    def send_inward(r):
+        for t in range(planes):
+
+            @pl.when(t <= z)
+            def _(t=t):
+                place_partials(t, 1 - c, r)
+                inward(t, r).start()
+
+        for t in range(planes):
+
+            @pl.when(t <= z)
+            def _(t=t):
+                place_partials(t, c, r)
+
+    def send_sideways(t, r):
         @pl.when(t <= z)
-        def _(t=t):
-            place_partials(t, 1 - c)
-            for k in kinds:
-                inward(t, k).start()
-
-    for t in range(planes):
-
-        @pl.when(t <= z)
-        def _(t=t):
-            place_partials(t, c)
-            for k in (1, 0) if t == 0 else (0, 1):
-                inward(t, k).wait_recv()
+        def _():
+            inward(t, r).wait_recv()
+            for k in (2 * r, 2 * r + 1):
                 away = part[t, c, k, 1 - y].astype(jnp.float32) + c_in[t, k, 1 - y].astype(jnp.float32)
                 held[t, k] = part[t, c, k, y].astype(jnp.float32) + c_in[t, k, y].astype(jnp.float32)
-                if (t, k) != (0, 0):
+                if t > 0 or k in late:
                     y_out[t, k] = away.astype(jnp.bfloat16)
                     sideways(t, k).start()
                 else:
 
                     @pl.when(z == planes - 1)
-                    def _():
+                    def _(k=k, away=away):
                         y_out[t, k] = away.astype(jnp.bfloat16)
-                        extra_down().start()
+                        extra_down(k).start()
                         z_out[t, k] = held[t, k].astype(jnp.bfloat16)
                         down(t, k).start()
 
                     @pl.when(z == planes - 2)
-                    def _():
-                        extra_down().wait_recv()
-                        y_out[t, k] = (away + extra_in[...].astype(jnp.float32)).astype(jnp.bfloat16)
+                    def _(k=k, away=away):
+                        extra_down(k).wait_recv()
+                        y_out[t, k] = (away + extra_in[k].astype(jnp.float32)).astype(jnp.bfloat16)
                         sideways(t, k).start()
 
                     @pl.when(z < planes - 2)
-                    def _():
+                    def _(k=k, away=away):
                         y_out[t, k] = away.astype(jnp.bfloat16)
                         sideways(t, k).start()
+
+    first = [(t, 0) for t in range(1, planes - 1)] + [(0, 0)]
+    second = [(0, 1), (planes - 1, 0)] + [(t, 1) for t in range(1, planes)]
+    chosen_gradients(0, 0)
+    chosen_gradients(1, 0)
+    send_inward(0)
+    chosen_gradients(0, 1)
+    for t, r in first:
+        send_sideways(t, r)
+    chosen_gradients(1, 1)
+    send_inward(1)
+    for h in range(heads):
+        dq[:, columns(h)] = (dq_sum[h] * SCALE).T.astype(jnp.bfloat16)
+    query_swap = toward(dq, dq_far, x_send.at[4], x_recv.at[4])
+    query_swap.start()
+    for t, r in second:
+        send_sideways(t, r)
 
     def dot(lhs, rhs):
         return lax.dot_general(lhs, rhs, NT, preferred_element_type=jnp.float32)
@@ -620,26 +648,29 @@
         total[:, here] = dot(dq[...], mine[here, :feature])
 
     tiles(project_query)
-    for copy in weights:
-        copy.wait_recv()
-    weight_swap.start()
-
     def project_query_far(here, there):
         total[:, here] += dot(dq_far[...], theirs[there[0], there[1], :feature])
 
-    for t in range(planes):
+    for t, r in [(t, 0) for t in range(planes - 1)] + second:
+        if (t, r) == second[0]:
+            for copy in weights:
+                copy.wait_recv()
+            weight_swap.start()
 
         @pl.when(t <= z)
-        def _(t=t):
-            @pl.when(t == z)
-            def _():
-                query_swap.wait()
-                weight_swap.wait()
-                tiles(project_query_far)
-
-            for k in kinds:
-
-                @pl.when((z < planes - 1) | ((t, k) != (0, 0)))
+        def _(t=t, r=r):
+            if r == 1:
+
+                @pl.when(t == z)
+                def _():
+                    query_swap.wait()
+                    weight_swap.wait()
+                    tiles(project_query_far)
+
+            for k in (2 * r, 2 * r + 1):
+                direct = t == 0 and k in early
+
+                @pl.when((z < planes - 1) | (not direct))
                 def _(k=k):
                     sideways(t, k).wait_recv()
                     held[t, k] += y_in[t, k].astype(jnp.float32)
@@ -649,21 +680,20 @@
                     down(t, k).wait_recv()
                     held[t, k] += z_in[t, k].astype(jnp.float32)
 
-                @pl.when((t < z) & ((z < planes - 1) | ((t, k) != (0, 0))))
+                @pl.when((t < z) & ((z < planes - 1) | (not direct)))
                 def _(k=k):
                     z_out[t, k] = held[t, k].astype(jnp.bfloat16)
                     down(t, k).start()
 
                 @pl.when(t == z)
                 def _(k=k):
-                    dkv[k] = held[t, k].astype(jnp.bfloat16)
+                    dkv[spot(k)] = held[t, k].astype(jnp.bfloat16)
                     keyval_swap(k).start()
 
     def project_keyval(here, there):
         summed[:, here] = (
             total[:, here]
-            + dot(dkv[0], mine[here, feature : feature + HD])
-            + dot(dkv[1], mine[here, feature + HD :])
+            + dot(dkv[...], mine[here, feature:])
         ).astype(jnp.bfloat16)
 
     tiles(project_keyval)
@@ -677,19 +707,20 @@
 
         @pl.when(z >= s)
         def _(s=s):
-            for k in kinds:
+            for r in range(2):
+                inward(s, r).wait_send()
+            for k in pieces:
                 if s < planes - 1:
 
                     @pl.when(z < planes - 1)
                     def _(k=k):
                         up(s, k).wait_send()
 
-                if (s, k) != (planes - 1, 1):
+                if s < planes - 1 or k in early:
                     across(s, k).wait_send()
                 between(s, k).wait_send()
-                inward(s, k).wait_send()
-
-                @pl.when((z < planes - 1) | ((s, k) != (0, 0)))
+
+                @pl.when((z < planes - 1) | (not (s == 0 and k in early)))
                 def _(k=k):
                     sideways(s, k).wait_send()
 
@@ -699,15 +730,17 @@
 
     @pl.when(z == planes - 2)
     def _():
-        extra_up().wait_send()
+        for k in late:
+            extra_up(k).wait_send()
 
     @pl.when(z == planes - 1)
     def _():
-        extra_down().wait_send()
+        for k in early:
+            extra_down(k).wait_send()
 
     for copy in weights:
         copy.wait_send()
-    for k in kinds:
+    for k in pieces:
         keyval_swap(k).wait()
     for copy in written:
         copy.wait()
@@ -716,8 +749,7 @@
 def finish_kernel(summed_ref, dkv_ref, far_ref, out_ref):
     out_ref[...] = (
         summed_ref[...].astype(jnp.float32)
-        + lax.dot_general(dkv_ref[0], far_ref[:, :HD], NT, preferred_element_type=jnp.float32)
-        + lax.dot_general(dkv_ref[1], far_ref[:, HD:], NT, preferred_element_type=jnp.float32)
+        + lax.dot_general(dkv_ref[...], far_ref[...], NT, preferred_element_type=jnp.float32)
     ).astype(jnp.bfloat16)
 
 
@@ -731,7 +763,7 @@
         grid=(half // wide,),
         in_specs=[
             column,
-            pl.BlockSpec(dkv_far.shape, lambda j: (0, 0, 0)),
+            pl.BlockSpec(dkv_far.shape, lambda j: (0, 0)),
             pl.BlockSpec((wide, far.shape[1]), lambda j: (j, 0)),
         ],
         out_specs=column,
@@ -754,34 +786,37 @@
     def full_type(*shape):
         return pltpu.VMEM(shape, jnp.float32)
 
-    slots = half_type(planes, 2, rows, HD)
+    piece = rows // 2
+    slots = half_type(planes, 4, piece, HD)
     summed, dkv_far, far = pl.pallas_call(
         functools.partial(fused_kernel, planes),
         out_shape=(
             jax.ShapeDtypeStruct((rows, half), jnp.bfloat16),
-            jax.ShapeDtypeStruct((2, rows, HD), jnp.bfloat16),
+            jax.ShapeDtypeStruct((rows, 2 * HD), jnp.bfloat16),
             jax.ShapeDtypeStruct((2, half // 2, 2 * HD), jnp.bfloat16),
         ),
         in_specs=[pl.BlockSpec(memory_space=pltpu.SMEM)] + [vmem] * 6 + [anywhere] * 3,
         out_specs=(anywhere,) * 3,
         scratch_shapes=[
-            half_type(planes, 2, 2, 2, rows, HD),
-            half_type(planes, 2, 2, 2, rows, HD),
+            half_type(planes, 2, 4, 2, piece, HD),
+            half_type(planes, 2, 4, 2, piece, HD),
             full_type(heads, rows),
-            full_type(2 * heads, HD, rows),
-            half_type(4, 2, rows, HD),
+            full_type(heads, HD, rows),
+            half_type(4, 4, piece, HD),
             half_type(rows, width),
             half_type(rows, width),
             half_type(half, features),
             half_type(2, half // 2, features),
             full_type(rows, half),
-            half_type(planes, 2, 2, rows, HD),
+            half_type(planes, 4, 2, piece, HD),
             slots, slots, slots, slots,
-            full_type(planes, 2, rows, HD),
-            half_type(2, rows, HD),
+            full_type(planes, 4, piece, HD),
+            half_type(rows, 2 * HD),
             half_type(rows, half),
-            half_type(rows, HD),
-        ] + [dma((planes, 2))] * 12 + [dma((3,)), dma((3,)), dma((3,)), dma(()), dma(()), dma((3,)), dma((3,)), dma((2,)), dma((2,)), dma((2,))],
+            half_type(2, piece, HD),
+        ] + [dma((planes, 4))] * 12 + [
+            dma((3,)), dma((3,)), dma((3,)), dma(()), dma(()), dma((5,)), dma((5,)), dma((4,)), dma((4,)), dma((2,)),
+        ],
         compiler_params=pltpu.CompilerParams(
             collective_id=2, has_side_effects=True, vmem_limit_bytes=VMEM_LIMIT
         ),

time: 70.5 us -> 75.5 us (1.071)
  Pallas kernels: 70.2 us -> 75.3 us
    pallas_call x1, Pallas kernels: 65.4 us -> 70.5 us  [fused(): pl.pallas_call(functools.partial(fused_kernel, planes), out_shape=(jax.Sh...]
where the time goes in v5:
time: 75.5 us; the launch traced here: 75.3 us
  Pallas kernels  75.3 us (100%)
    pallas_call x1, Pallas kernels, fused(): pl.pallas_call(functools.partial(fused_kernel, planes), out_shape=(jax.Sh...  70.5 us
    pallas_call x1, Pallas kernels, finish(): pl.pallas_call(finish_kernel, out_shape=jax.ShapeDtypeStruct(summed.shape...  4.79 us

profile of v5, /device:TPU:0, one launch (start us, length us, event | category | flops | bytes accessed | tf_op | source)
XLA Modules:
  0.0 75.3 jit_solution(7396457371988970428)
XLA Ops:
  0.0 70.5 %fused.1 = (bf16[512,2048]{1,0:T(8,128)(2,1)}, bf16[512,256]{1,0:T(8,128)(2,1)}, bf16[2,1024,256]{2,1,0:T(8,128)(2,1)}) custom-call(s32[3,16]{1,0:T(4,128)} %bitcast.5, bf16[512,128]{1,0:T(8,128)(2,1)} %key_ref.1, bf16[512,128]{1,0:T(8,128)(2,1)} %value_ref.1, bf16[512,512]{1,0:T(8,128)(2,1)} %q_ref.1, bf16[512,512]{1,0:T(8,128)(2,1)} %do_ref.1, ...), custom_call_target="tpu_custom_call" | custom-call | tf_op jit(solution)/shard_map/fused/pallas_call | solution.py:791
  70.5 4.8 %finish.1 = bf16[512,2048]{1,0:T(8,128)(2,1)} custom-call(bf16[512,2048]{1,0:T(8,128)(2,1)} %get-tuple-element.8.summed_ref, bf16[512,256]{1,0:T(8,128)(2,1)} %get-tuple-element.9.dkv_ref, bf16[2048,256]{1,0:T(8,128)(2,1)} %bitcast.3), custom_call_target="tpu_custom_call" | custom-call | tf_op jit(solution)/shard_map/finish/pallas_call | solution.py:760

commit v6 on v4

--- a/solution.py
+++ b/solution.py
@@ -620,10 +620,6 @@
         total[:, here] = dot(dq[...], mine[here, :feature])
 
     tiles(project_query)
-    for copy in weights:
-        copy.wait_recv()
-    weight_swap.start()
-
     def project_query_far(here, there):
         total[:, here] += dot(dq_far[...], theirs[there[0], there[1], :feature])
 
@@ -631,6 +627,12 @@
 
         @pl.when(t <= z)
         def _(t=t):
+            @pl.when(t == jnp.minimum(z, 1))
+            def _():
+                for copy in weights:
+                    copy.wait_recv()
+                weight_swap.start()
+
             @pl.when(t == z)
             def _():
                 query_swap.wait()

time: 70.5 us -> 74.5 us (1.057)
  the two profiles are of different devices: /device:TPU:0 before, /device:TPU:12 now
where the time goes in v6:
time: 74.5 us; the launch traced here: 74.3 us
  Pallas kernels  74.3 us (100%)
    pallas_call x1, Pallas kernels, fused(): pl.pallas_call(functools.partial(fused_kernel, planes), out_shape=(jax.Sh...  69.5 us
    pallas_call x1, Pallas kernels, finish(): pl.pallas_call(finish_kernel, out_shape=jax.ShapeDtypeStruct(summed.shape...  4.84 us

profile of v6, /device:TPU:12, one launch (start us, length us, event | category | flops | bytes accessed | tf_op | source)
XLA Modules:
  0.0 74.3 jit_solution(3979632469490976552)
XLA Ops:
  0.0 69.5 %fused.1 = (bf16[512,2048]{1,0:T(8,128)(2,1)}, bf16[2,512,128]{2,1,0:T(8,128)(2,1)}, bf16[2,1024,256]{2,1,0:T(8,128)(2,1)}) custom-call(s32[3,16]{1,0:T(4,128)} %bitcast.5, bf16[512,128]{1,0:T(8,128)(2,1)} %key_ref.1, bf16[512,128]{1,0:T(8,128)(2,1)} %value_ref.1, bf16[512,512]{1,0:T(8,128)(2,1)} %q_ref.1, bf16[512,512]{1,0:T(8,128)(2,1)} %do_ref.1, ...), custom_call_target="tpu_custom_call" | custom-call | tf_op jit(solution)/shard_map/fused/pallas_call | solution.py:760
  69.5 4.8 %finish.1 = bf16[512,2048]{1,0:T(8,128)(2,1)} custom-call(bf16[512,2048]{1,0:T(8,128)(2,1)} %get-tuple-element.8.summed_ref, bf16[2,512,128]{2,1,0:T(8,128)(2,1)} %get-tuple-element.9.dkv_ref, bf16[2048,256]{1,0:T(8,128)(2,1)} %bitcast.3), custom_call_target="tpu_custom_call" | custom-call | tf_op jit(solution)/shard_map/finish/pallas_call | solution.py:730
